TPU v7x, 256 devices: a whole 4x4x8 slice. The times are simulated.
256 devices in a mesh: src: 16 (over z, y_lo), row: 16 (over x, y_hi, core).
Axes of the slice: x: 4, y: 4 (y_hi: 2, y_lo: 2; y = y_hi * 2 + y_lo), z: 8, core: 2. Of those that a mesh axis runs over, the one named last changes fastest.
Arguments:
- pupil: float32 [2, 1024, 1024], P(None, None, 'row'), may hold values from -6 to 6
- mask_spectrum: bfloat16 [2, 1088, 1024], P(None, None, 'row'), may hold values from -6 to 6
- shifts: int32 [32, 2], P('src'), may hold values from 0 to 63, as said below
- weights: float32 [32], P('src'), may hold values from 0.25 to 1
- measured: float32 [1024, 4096], P('row'), may hold values from 0.5 to 5
Outputs:
- pupil_grad: float32 [2, 1024, 1024], P(None, 'src', 'row')
- intensity: float32 [1024, 4096], P('row', 'src')
Inputs may be any that keep to these rules, and one draw needn't show every extreme that they name: `shifts`: column 0 is a row offset, column 1 a column offset; each column takes the value 0 at some source point and 63 at some source point.
All inputs are finite; a program needn't handle non-finite values.
Results may differ from a plain program's by a relative error of at most 0.0061.
Values may be sent and summed in bfloat16 or wider, within the bound.
No kernel may reach another device: no remote copies, remote signals or barrier semaphores. Data moves between devices by JAX's collectives and lax.ppermute only.
A program may use at most 192 MiB of HBM per device.

v0:
```python
import math

import jax
import jax.numpy as jnp
from jax import lax
from jax.sharding import PartitionSpec as P

K = 1024
NC = 4096
R_DEV = 64
SRC_DEV = 2


def passed_along(block, axis, distance):
    devices = range(lax.axis_size(axis))
    route = [(i - distance, i) for i in devices if i - distance in devices]
    return lax.ppermute(block, axis, route)


def phase_tables(first_pos, pos_count, freq_count, period):
    positions = first_pos + lax.iota(jnp.int32, pos_count)
    frequency = lax.iota(jnp.int32, freq_count) - freq_count // 2
    turn_count = jnp.mod(positions[:, None] * frequency[None, :], period)
    phase_angle = turn_count.astype(jnp.float32) * (2.0 * math.pi / period)
    return (jnp.cos(phase_angle).astype(jnp.bfloat16), jnp.sin(phase_angle).astype(jnp.bfloat16))


def shards(pupil, mask_spectrum, shifts, weights, measured):
    slab_width = pupil.shape[2]
    full_rows = R_DEV * lax.axis_size("row")
    sources = SRC_DEV * lax.axis_size("src")
    col_width = min(512, NC)
    beyond = passed_along(mask_spectrum, "row", -1)
    wide_mask = jnp.concatenate([mask_spectrum, beyond], axis=2)
    windows = jnp.stack(
        [
            lax.dynamic_slice(
                wide_mask, (0, shifts[member, 0], shifts[member, 1]), (2, K, slab_width)
            )
            for member in range(SRC_DEV)
        ]
    ).astype(jnp.float32)
    mask_real = windows[:, 0]
    mask_imag = windows[:, 1]
    field_in = jnp.stack(
        [pupil[0] * mask_real - pupil[1] * mask_imag, pupil[0] * mask_imag + pupil[1] * mask_real],
        axis=1,
    ).astype(jnp.bfloat16)
    cosine_rows, sine_rows = phase_tables(0, full_rows, K, NC)
    along_cos = jnp.einsum(
        "xf,scfk->scxk", cosine_rows, field_in, preferred_element_type=jnp.float32
    )
    along_sin = jnp.einsum("xf,scfk->scxk", sine_rows, field_in, preferred_element_type=jnp.float32)
    row_parts = (
        jnp.stack([along_cos[:, 0] - along_sin[:, 1], along_cos[:, 1] + along_sin[:, 0]], axis=1)
        * (1.0 / K)
    ).astype(jnp.bfloat16)

    def forward_rows(exchanged):
        item_count = exchanged.shape[0]
        local_rows = exchanged.shape[2]
        flat_rows = exchanged.reshape(item_count * 2 * local_rows, K)
        pieces = []
        for col_start in range(0, NC, col_width):
            cosine_cols, sine_cols = phase_tables(col_start, col_width, K, NC)
            with_cos = jnp.einsum(
                "rf,yf->ry", flat_rows, cosine_cols, preferred_element_type=jnp.float32
            ).reshape(item_count, 2, local_rows, col_width)
            with_sin = jnp.einsum(
                "rf,yf->ry", flat_rows, sine_cols, preferred_element_type=jnp.float32
            ).reshape(item_count, 2, local_rows, col_width)
            pieces.append(
                jnp.stack(
                    [with_cos[:, 0] - with_sin[:, 1], with_sin[:, 0] + with_cos[:, 1]], axis=1
                )
            )
        return jnp.concatenate(pieces, axis=3)

    fields = jnp.concatenate(
        [
            forward_rows(
                lax.all_to_all(
                    row_parts[member : member + 1], "row", split_axis=2, concat_axis=3, tiled=True
                )
            )
            for member in range(SRC_DEV)
        ],
        axis=0,
    )
    partial_image = jnp.sum(
        weights[:, None, None]
        * (fields[:, 0] * fields[:, 0] + fields[:, 1] * fields[:, 1])
        / sources,
        axis=0,
    )
    col_share = NC // lax.axis_size("src")
    col_first = lax.axis_index("src") * col_share
    summed = lax.psum(partial_image, "src")
    intensity = lax.dynamic_slice_in_dim(summed, col_first, col_share, 1)
    residual = summed - measured
    grad_scale = 2.0 / math.sqrt(sources * full_rows * NC)
    factor = grad_scale * weights[:, None, None, None] * residual[None, None]
    flat_scaled = (factor * fields).astype(jnp.bfloat16).reshape(SRC_DEV * 2 * R_DEV, NC)
    back_real = jnp.zeros((SRC_DEV, R_DEV, K), jnp.float32)
    back_imag = jnp.zeros((SRC_DEV, R_DEV, K), jnp.float32)
    for col_start in range(0, NC, col_width):
        cosine_cols, sine_cols = phase_tables(col_start, col_width, K, NC)
        scaled_block = flat_scaled[:, col_start : col_start + col_width]
        with_cos = jnp.einsum(
            "ry,yf->rf", scaled_block, cosine_cols, preferred_element_type=jnp.float32
        ).reshape(SRC_DEV, 2, R_DEV, K)
        with_sin = jnp.einsum(
            "ry,yf->rf", scaled_block, sine_cols, preferred_element_type=jnp.float32
        ).reshape(SRC_DEV, 2, R_DEV, K)
        back_real = back_real + with_cos[:, 0] + with_sin[:, 1]
        back_imag = back_imag + with_cos[:, 1] - with_sin[:, 0]
    col_parts = jnp.stack([back_real, back_imag], axis=1).astype(jnp.bfloat16)

    def backward_rows(exchanged):
        back_cos = jnp.einsum(
            "xf,scxk->scfk", cosine_rows, exchanged, preferred_element_type=jnp.float32
        )
        back_sin = jnp.einsum(
            "xf,scxk->scfk", sine_rows, exchanged, preferred_element_type=jnp.float32
        )
        return jnp.stack([back_cos[:, 0] + back_sin[:, 1], back_cos[:, 1] - back_sin[:, 0]], axis=1)

    spectra = jnp.concatenate(
        [
            backward_rows(
                lax.all_to_all(
                    col_parts[member : member + 1], "row", split_axis=3, concat_axis=2, tiled=True
                )
            )
            for member in range(SRC_DEV)
        ],
        axis=0,
    )
    grad_real = jnp.sum(mask_real * spectra[:, 0] + mask_imag * spectra[:, 1], axis=0)
    grad_imag = jnp.sum(mask_real * spectra[:, 1] - mask_imag * spectra[:, 0], axis=0)
    pupil_grad = lax.psum_scatter(
        jnp.stack([grad_real, grad_imag]), "src", scatter_dimension=1, tiled=True
    )
    return (pupil_grad, intensity)


def solution(mesh):
    return jax.shard_map(
        shards,
        mesh=mesh,
        in_specs=(
            P(None, None, "row"),
            P(None, None, "row"),
            P("src", None),
            P("src"),
            P("row", None),
        ),
        out_specs=(P(None, "src", "row"), P("row", "src")),
        check_vma=False,
    )
```

profile of v0, /device:TPU:2, one launch (start us, length us, event | category | flops | bytes accessed | tf_op | source)
XLA Modules:
  0.0 967.3 jit_solution(4982597307561561800)
XLA Ops:
  23.4 15.9 %fusion.59 = f32[2,2,1024,64]{2,3,1,0:T(8,128)S(1)} fusion(s32[1024]{0:T(1024)S(1)} %iota_add_fusion, bf16[2,1,1024,64]{2,3,1,0:T(8,128)(2,1)S(1)} %get-tuple-element.13, bf16[2,1,1024,64]{2,3,1,0:T(8,128)(2,1)S(1)} %get-tuple-element.12), kind=kOutput, calls=%fused_computation.121 | convolution fusion | flops 552861696 | bytes 1576960 | tf_op jit(solution)/shard_map/xf,scfk->scxk/dot_general | solution.py:53
  39.3 16.0 %fusion.56 = f32[2,2,1024,64]{2,3,1,0:T(8,128)S(1)} fusion(s32[1024]{0:T(1024)S(1)} %iota_add_fusion, bf16[2,1,1024,64]{2,3,1,0:T(8,128)(2,1)S(1)} %get-tuple-element.13, bf16[2,1,1024,64]{2,3,1,0:T(8,128)(2,1)S(1)} %get-tuple-element.12), kind=kOutput, calls=%fused_computation.120 | convolution fusion | flops 552861696 | bytes 1576960 | tf_op jit(solution)/shard_map/xf,scfk->scxk/dot_general | solution.py:50
  83.8 9.0 convolution_bitcast_fusion.28
  92.9 8.7 convolution_bitcast_fusion.29
  101.6 9.1 convolution_bitcast_fusion.26
  110.6 8.7 convolution_bitcast_fusion.27
  119.4 9.3 convolution_bitcast_fusion.24
  128.6 8.7 convolution_bitcast_fusion.25
  137.4 9.0 convolution_bitcast_fusion.22
  146.4 8.9 convolution_bitcast_fusion.23
  163.2 9.2 convolution_bitcast_fusion.21
  180.3 8.0 convolution_bitcast_fusion.19
  188.3 8.1 convolution_bitcast_fusion.16
  204.3 8.2 convolution_bitcast_fusion.31
  213.5 8.0 convolution_bitcast_fusion.14
  229.3 8.1 convolution_bitcast_fusion.12
  237.4 8.2 convolution_bitcast_fusion.13
  253.6 8.0 convolution_bitcast_fusion.11
  261.6 8.1 convolution_bitcast_fusion.8
  277.5 8.3 convolution_bitcast_fusion.6
  285.8 8.0 convolution_bitcast_fusion.7
  301.7 8.0 convolution_bitcast_fusion.5
  309.8 8.3 convolution_bitcast_fusion.2
  325.9 8.1 convolution_bitcast_fusion
  334.0 8.0 convolution_bitcast_fusion.1
  347.3 142.6 %all-reduce.2.cloned.1.call-done = f32[64,4096]{1,0:T(8,128)} async-done(((f32[64,4096]{1,0:T(8,128)}), f32[64,4096]{1,0:T(8,128)}) %all-reduce.2.cloned.1.call-update) | async-done | bytes 1048592 | tf_op jit(solution)/shard_map/psum | solution.py:98
  493.2 8.3 fusion.122
  501.5 8.9 fusion.121
  510.4 9.1 fusion.120
  519.5 9.1 fusion.119
  528.6 8.9 fusion.118
  537.5 9.3 fusion.117
  546.8 9.1 fusion.116
  555.9 8.9 fusion.115
  564.8 9.2 fusion.114
  574.0 9.2 fusion.113
  583.2 8.9 fusion.112
  592.2 9.0 fusion.111
  601.2 9.1 fusion.110
  610.3 8.8 fusion.109
  619.1 9.3 fusion.107
  628.4 8.9 fusion.108
  778.2 9.6 add_convert_fusion
  819.3 16.2 %fusion.71 = f32[1,2,1024,64]{2,3,1,0:T(8,128)S(1)} fusion(bf16[2,1024,64]{1,2,0:T(8,128)(2,1)S(1)} %reshape.523, s32[1024]{0:T(1024)S(1)} %iota_add_fusion), kind=kOutput, calls=%fused_computation.125 | convolution fusion | flops 284164096 | bytes 790528 | tf_op jit(solution)/shard_map/xf,scxk->scfk/dot_general | solution.py:123
  835.6 15.9 %fusion.65 = f32[1,2,1024,64]{2,3,1,0:T(8,128)S(1)} fusion(bf16[2,1024,64]{1,2,0:T(8,128)(2,1)S(1)} %reshape.523, s32[1024]{0:T(1024)S(1)} %iota_add_fusion), kind=kOutput, calls=%fused_computation.123 | convolution fusion | flops 284164096 | bytes 790528 | tf_op jit(solution)/shard_map/xf,scxk->scfk/dot_general | solution.py:120
  852.5 16.3 %fusion.68 = f32[1,2,1024,64]{2,3,1,0:T(8,128)S(1)} fusion(bf16[2,1024,64]{1,2,0:T(8,128)(2,1)S(1)} %reshape.522, s32[1024]{0:T(1024)S(1)} %iota_add_fusion), kind=kOutput, calls=%fused_computation.124 | convolution fusion | flops 284164096 | bytes 790528 | tf_op jit(solution)/shard_map/xf,scxk->scfk/dot_general | solution.py:123
  868.8 15.9 %fusion.62 = f32[1,2,1024,64]{2,3,1,0:T(8,128)S(1)} fusion(bf16[2,1024,64]{1,2,0:T(8,128)(2,1)S(1)} %reshape.522, s32[1024]{0:T(1024)S(1)} %iota_add_fusion), kind=kOutput, calls=%fused_computation.122 | convolution fusion | flops 284164096 | bytes 790528 | tf_op jit(solution)/shard_map/xf,scxk->scfk/dot_general | solution.py:120
  889.8 68.7 %reduce-scatter.4.cloned.1.call-done = f32[64,128]{1,0:T(8,128)} async-done(((f32[1024,128]{1,0:T(8,128)}), f32[64,128]{1,0:T(8,128)}) %reduce-scatter.4.cloned.1.call-update) | async-done | bytes 32784
  (217 shorter events, 288.8 us)
Async XLA Ops:
  7.2 15.6 %collective-permute-start = (bf16[2,1088,64]{1,2,0:T(8,128)(2,1)}, bf16[2,1088,64]{1,2,0:T(8,128)(2,1)S(1)}, u32[]{:S(2)}, u32[]{:S(2)}) collective-permute-start(bf16[2,1088,64]{1,2,0:T(8,128)(2,1)} %param.6), channel_id=1, source_target_pairs={{1,0},{2,1},{3,2},{4,3},{5,4},{6,5},{7,6},{8,7},{9,8},{10,9},{11,1... | collective-permute-start | bytes 835592 | tf_op jit(solution)/shard_map/ppermute | solution.py:17
  23.2 16.1 %copy-start.2 = (f32[2,2,1024,64]{2,3,1,0:T(8,128)}, f32[2,2,1024,64]{2,3,1,0:T(8,128)S(1)}, u32[]{:S(2)}) copy-start(f32[2,2,1024,64]{2,3,1,0:T(8,128)S(1)} %maximum_convert_fusion) | copy-start | bytes 3145732
  57.1 12.0 %all-to-all-start = ((bf16[16,2,4096]{2,1,0:T(2,128)(2,1)}), bf16[16,2,4096]{2,1,0:T(2,128)(2,1)S(1)}, u32[]{:S(2)}, u32[]{:S(2)}) async-start(bf16[16,2,4096]{2,1,0:T(2,128)(2,1)} %reshape.548), calls=%async_computation | async-start | bytes 524288 | tf_op jit(solution)/shard_map/all_to_all | solution.py:82
  69.1 143.4 %all-to-all-start.1 = ((bf16[16,2,4096]{2,1,0:T(2,128)(2,1)}), bf16[16,2,4096]{2,1,0:T(2,128)(2,1)S(1)}, u32[]{:S(2)}, u32[]{:S(2)}) async-start(bf16[16,2,4096]{2,1,0:T(2,128)(2,1)} %reshape.546), calls=%async_computation.1 | async-start | bytes 524288 | tf_op jit(solution)/shard_map/all_to_all | solution.py:82
  74.7 415.1 %all-reduce.2.cloned.1.call-start = ((), (), s32[]{:S(2)}) async-start(), calls=%async_computation.5 | async-start | bytes 2097152 | tf_op jit(solution)/shard_map/psum | solution.py:98
  334.0 8.2 copy-start.28
  334.0 8.2 copy-start.29
  342.0 1.0 copy-start.26
  342.0 1.0 copy-start.27
  342.0 1.1 copy-start.24
  342.1 1.2 copy-start.25
  342.1 1.2 copy-start.22
  342.1 1.3 copy-start.23
  342.1 1.4 copy-start.21
  344.1 1.5 copy-start.30
  344.4 1.3 copy-start
  345.7 144.1 %copy-start.20 = (f32[64,4096]{1,0:T(8,128)S(1)}, f32[64,4096]{1,0:T(8,128)}, u32[]{:S(2)}) copy-start(f32[64,4096]{1,0:T(8,128)} %param.9) | copy-start | bytes 3145732
  491.2 1.6 copy-start.1
  778.1 9.8 %copy-start.4 = (f32[2,1,64,1024]{2,1,0,3:T(1,128)S(1)}, f32[2,1,64,1024]{2,1,0,3:T(1,128)}, u32[]{:S(2)}) copy-start(f32[2,1,64,1024]{2,1,0,3:T(1,128)} %copy.125) | copy-start | bytes 1572868
  778.1 9.8 %copy-start.5 = (f32[2,1,64,1024]{2,1,0,3:T(1,128)S(1)}, f32[2,1,64,1024]{2,1,0,3:T(1,128)}, u32[]{:S(2)}) copy-start(f32[2,1,64,1024]{2,1,0,3:T(1,128)} %copy.124) | copy-start | bytes 1572868
  778.1 9.8 %copy-start.6 = (f32[2,1,64,1024]{2,1,0,3:T(1,128)S(1)}, f32[2,1,64,1024]{2,1,0,3:T(1,128)}, u32[]{:S(2)}) copy-start(f32[2,1,64,1024]{2,1,0,3:T(1,128)} %copy.123) | copy-start | bytes 1572868
  778.1 9.8 %copy-start.7 = (f32[2,1,64,1024]{2,1,0,3:T(1,128)S(1)}, f32[2,1,64,1024]{2,1,0,3:T(1,128)}, u32[]{:S(2)}) copy-start(f32[2,1,64,1024]{2,1,0,3:T(1,128)} %copy.122) | copy-start | bytes 1572868
  778.1 9.8 %copy-start.8 = (f32[2,1,64,1024]{2,1,0,3:T(1,128)S(1)}, f32[2,1,64,1024]{2,1,0,3:T(1,128)}, u32[]{:S(2)}) copy-start(f32[2,1,64,1024]{2,1,0,3:T(1,128)} %copy.121) | copy-start | bytes 1572868
  778.1 9.8 %copy-start.9 = (f32[2,1,64,1024]{2,1,0,3:T(1,128)S(1)}, f32[2,1,64,1024]{2,1,0,3:T(1,128)}, u32[]{:S(2)}) copy-start(f32[2,1,64,1024]{2,1,0,3:T(1,128)} %copy.120) | copy-start | bytes 1572868
  778.1 9.8 %copy-start.10 = (f32[2,1,64,1024]{2,1,0,3:T(1,128)S(1)}, f32[2,1,64,1024]{2,1,0,3:T(1,128)}, u32[]{:S(2)}) copy-start(f32[2,1,64,1024]{2,1,0,3:T(1,128)} %copy.119) | copy-start | bytes 1572868
  778.1 9.8 %copy-start.11 = (f32[2,1,64,1024]{2,1,0,3:T(1,128)S(1)}, f32[2,1,64,1024]{2,1,0,3:T(1,128)}, u32[]{:S(2)}) copy-start(f32[2,1,64,1024]{2,1,0,3:T(1,128)} %copy.118) | copy-start | bytes 1572868
  778.1 9.8 %copy-start.12 = (f32[2,1,64,1024]{2,1,0,3:T(1,128)S(1)}, f32[2,1,64,1024]{2,1,0,3:T(1,128)}, u32[]{:S(2)}) copy-start(f32[2,1,64,1024]{2,1,0,3:T(1,128)} %copy.117) | copy-start | bytes 1572868
  778.2 9.8 %copy-start.13 = (f32[2,1,64,1024]{2,1,0,3:T(1,128)S(1)}, f32[2,1,64,1024]{2,1,0,3:T(1,128)}, u32[]{:S(2)}) copy-start(f32[2,1,64,1024]{2,1,0,3:T(1,128)} %copy.116) | copy-start | bytes 1572868
  778.2 9.8 %copy-start.14 = (f32[2,1,64,1024]{2,1,0,3:T(1,128)S(1)}, f32[2,1,64,1024]{2,1,0,3:T(1,128)}, u32[]{:S(2)}) copy-start(f32[2,1,64,1024]{2,1,0,3:T(1,128)} %copy.115) | copy-start | bytes 1572868
  778.2 9.8 %copy-start.15 = (f32[2,1,64,1024]{2,1,0,3:T(1,128)S(1)}, f32[2,1,64,1024]{2,1,0,3:T(1,128)}, u32[]{:S(2)}) copy-start(f32[2,1,64,1024]{2,1,0,3:T(1,128)} %copy.114) | copy-start | bytes 1572868
  778.2 9.8 %copy-start.16 = (f32[2,1,64,1024]{2,1,0,3:T(1,128)S(1)}, f32[2,1,64,1024]{2,1,0,3:T(1,128)}, u32[]{:S(2)}) copy-start(f32[2,1,64,1024]{2,1,0,3:T(1,128)} %copy.113) | copy-start | bytes 1572868
  778.2 9.8 %copy-start.17 = (f32[2,1,64,1024]{2,1,0,3:T(1,128)S(1)}, f32[2,1,64,1024]{2,1,0,3:T(1,128)}, u32[]{:S(2)}) copy-start(f32[2,1,64,1024]{2,1,0,3:T(1,128)} %copy.112) | copy-start | bytes 1572868
  778.2 9.8 %copy-start.18 = (f32[2,1,64,1024]{2,1,0,3:T(1,128)S(1)}, f32[2,1,64,1024]{2,1,0,3:T(1,128)}, u32[]{:S(2)}) copy-start(f32[2,1,64,1024]{2,1,0,3:T(1,128)} %copy.110) | copy-start | bytes 1572868
  778.2 9.8 %copy-start.19 = (f32[2,1,64,1024]{2,1,0,3:T(1,128)S(1)}, f32[2,1,64,1024]{2,1,0,3:T(1,128)}, u32[]{:S(2)}) copy-start(f32[2,1,64,1024]{2,1,0,3:T(1,128)} %copy.111) | copy-start | bytes 1572868
  798.2 14.4 %all-to-all-start.3 = ((bf16[16,2,4096]{2,1,0:T(2,128)(2,1)}), bf16[16,2,4096]{2,1,0:T(2,128)(2,1)S(1)}, u32[]{:S(2)}, u32[]{:S(2)}) async-start(bf16[16,2,4096]{2,1,0:T(2,128)(2,1)} %reshape.550), calls=%async_computation.3 | async-start | bytes 524288 | tf_op jit(solution)/shard_map/all_to_all | solution.py:131
  812.6 38.8 %all-to-all-start.2 = ((bf16[16,2,4096]{2,1,0:T(2,128)(2,1)}), bf16[16,2,4096]{2,1,0:T(2,128)(2,1)S(1)}, u32[]{:S(2)}, u32[]{:S(2)}) async-start(bf16[16,2,4096]{2,1,0:T(2,128)(2,1)} %reshape.552), calls=%async_computation.2 | async-start | bytes 524288 | tf_op jit(solution)/shard_map/all_to_all | solution.py:131
  818.2 140.3 %reduce-scatter.4.cloned.1.call-start = ((), (), s32[]{:S(2)}) async-start(), calls=%async_computation.6 | async-start | bytes 557056
  884.8 1.2 copy-start.3
Sparse Core Ops, SparseCore 0:
  347.4 142.4 all-reduce.1
  888.5 70.0 reduce-scatter.3
where the time goes:
time: 979 us; the launch traced here: 967 us
  matrix products  505 us (52%)
  waiting for transfers between devices  223 us (23%)
  local copies, waits for them, and re-layouts  164 us (17%)
  starting transfers between devices  28.3 us (3%)
  other arithmetic  24.2 us (2%)
  between operations  23.1 us (2%)
    psum x1, waiting for transfers between devices, shards(): summed = lax.psum(partial_image, 'src')  143 us
    dot_general x16, matrix products, forward_rows(): jnp.einsum('rf,yf->ry', flat_rows, sine_cols, preferred_element_type=jnp....  133 us
    dot_general x16, matrix products, forward_rows(): jnp.einsum('rf,yf->ry', flat_rows, cosine_cols, preferred_element_type=jn...  132 us
    unnamed x107, local copies, waits for them, and re-layouts  121 us
    dot_general x8, matrix products, shards(): jnp.einsum('ry,yf->rf', scaled_block, cosine_cols, preferred_element_type...  72.5 us
    dot_general x8, matrix products, shards(): jnp.einsum('ry,yf->rf', scaled_block, sine_cols, preferred_element_type=j...  71.6 us
    unnamed x3, waiting for transfers between devices  68.8 us
    slice x16, local copies, waits for them, and re-layouts, shards(): back_real = back_real + with_cos[:, 0] + with_sin[:, 1]  35.3 us
  transfers between devices with their start and end apart: 7, of which 4 were waited for; matrix products, arithmetic and copies ran while one was open for 18% of the time, Pallas kernels for 0%

commit v1 on v0

v1 whole, which is shorter than its diff:
```python
import functools
import math

import jax
import jax.numpy as jnp
import ml_dtypes
import numpy as np
from jax import lax
from jax.experimental import pallas as pl
from jax.experimental.pallas import tpu as pltpu
from jax.sharding import Mesh, PartitionSpec as P

K = 1024
NC = 4096
NR = 1024
SOURCES = 32
SH = 64
NZ = 8
NYL = 2
NROW = 16
DEST = NYL * NROW
GRAD_SCALE = 2.0 / math.sqrt(SOURCES * NR * NC)
VMEM_LIMIT = 56 * 1024 * 1024
F32 = jnp.float32
BF16 = jnp.bfloat16
NT = (((1,), (1,)), ((), ()))
TN = (((0,), (0,)), ((), ()))


def phase(position, frequency):
    turns = np.mod(position * frequency, NC).astype(np.float32)
    angle = turns * np.float32(2.0 * math.pi / NC)
    return np.cos(angle), np.sin(angle)


@functools.cache
def row_tables():
    z, i, yl, row = np.meshgrid(np.arange(NZ), np.arange(4), np.arange(NYL), np.arange(NROW), indexing="ij")
    x = (64 * row + 8 * z + 4 * yl + i).reshape(NZ, 128, 1)
    cosine, sine = phase(x, np.arange(K) - K // 2)
    return np.concatenate([cosine, sine], axis=1).astype(ml_dtypes.bfloat16)


@functools.cache
def col_tables():
    f0, q, rr, k1 = np.meshgrid(np.arange(4), np.arange(4), np.arange(4), np.arange(16), indexing="ij")
    f = (64 * (4 * q + rr) + 4 * k1 + f0 - K // 2).reshape(4, 4, 64, 1)
    cosine, sine = phase(f, np.arange(1024))
    return np.stack([cosine, sine], axis=2).reshape(4, 512, 1024).astype(ml_dtypes.bfloat16)


@functools.cache
def lane_order():
    rr, c, k = np.meshgrid(np.arange(4), np.arange(2), np.arange(64), indexing="ij")
    target = (k % 4) * 128 + c * 64 + rr * 16 + k // 4
    order = np.zeros((512, 512), np.float32)
    order[np.arange(512), target.reshape(-1)] = 1.0
    return order.astype(ml_dtypes.bfloat16)


def lane_sign(shape):
    lane = lax.broadcasted_iota(jnp.int32, shape, len(shape) - 1)
    return jnp.where((lane & 127) < 64, 1.0, -1.0).astype(F32)


def rows_kernel(scal, table, here, beyond, pupil, out, windows, mask, wide, field, sums):
    mask[...] = jnp.concatenate([here[...], beyond[...]], axis=2)
    column = lax.broadcasted_iota(jnp.int32, (64, 128), 1) - lax.broadcasted_iota(jnp.int32, (64, 128), 0)
    lane = lax.broadcasted_iota(jnp.int32, (64, 128), 1)
    sign = -lane_sign((128, 128))

    def group(g, carry):
        picks = []
        for m in range(4):
            b = scal[2 * g + m // 2, 3 * (m % 2) + 1].astype(jnp.int32)
            picks.append(jnp.where(column == b, 1.0, 0.0).astype(BF16))
        pick = jnp.concatenate(picks, axis=0)
        for c in range(2):
            wide[c, :, : K + SH] = lax.dot_general(pick, mask[c], NT, preferred_element_type=F32)
        for m in range(4):
            a = scal[2 * g + m // 2, 3 * (m % 2)].astype(jnp.int32)
            rows = slice(m * 64, (m + 1) * 64)
            turn = (128 - a) & 127
            keep = lane < 128 - a
            rolled = [
                pltpu.roll(wide[c, rows, 0:128], turn, 1) for c in range(2)
            ]
            for t in range(8):
                cols = slice(t * 128, (t + 1) * 128)
                after = slice((t + 1) * 128, (t + 2) * 128)
                following = [pltpu.roll(wide[c, rows, after], turn, 1) for c in range(2)]
                wr, wi = [jnp.where(keep, rolled[c], following[c]) for c in range(2)]
                rolled = following
                pr, pi = pupil[0, :, cols], pupil[1, :, cols]
                field[m * 128 : m * 128 + 64, cols] = (pr * wr - pi * wi).astype(BF16)
                field[m * 128 + 64 : m * 128 + 128, cols] = (pr * wi + pi * wr).astype(BF16)
                windows[4 * g + m, 0:64, cols] = wr.astype(BF16)
                windows[4 * g + m, 64:128, cols] = wi.astype(BF16)
        for pair in range(2):
            both = lax.dot_general(
                table[...], field[pair * 256 : (pair + 1) * 256, :], NT, preferred_element_type=F32
            )
            for n in range(2):
                m = 2 * pair + n
                root = scal[2 * g + pair, 3 * n + 2] * (1.0 / K)
                by_cos = both[:128, n * 128 : (n + 1) * 128]
                by_sin = both[128:, n * 128 : (n + 1) * 128]
                mixed = (by_cos + sign * pltpu.roll(by_sin, 64, 1)) * root
                for i in range(4):
                    sums[pl.ds((4 * g + m) * 4 + i, 32, stride=64), :] = mixed[i * 32 : (i + 1) * 32]
        return carry

    lax.fori_loop(0, 4, group, 0)
    out[...] = sums[...].reshape(DEST, 64, 128).astype(BF16)


def image_kernel(x, order, table, measured, y, intensity, left, back, parts):
    sign = lane_sign((128, 128))
    for q in range(4):
        lined = jnp.concatenate(
            [jnp.concatenate([x[yl * 16 + 4 * q + rr] for yl in range(2)], axis=0) for rr in range(4)], axis=1
        )
        sorted_lanes = jnp.dot(lined, order[...], preferred_element_type=F32)
        for f0 in range(4):
            tile = sorted_lanes[:, f0 * 128 : (f0 + 1) * 128]
            left[f0, 0:128, q * 128 : (q + 1) * 128] = (tile * sign).astype(BF16)
            left[f0, 128:256, q * 128 : (q + 1) * 128] = pltpu.roll(tile, 64, 1).astype(BF16)

    upper = lax.broadcasted_iota(jnp.int32, (8, 128), 0) < 4
    for n in range(4):
        cols = slice(n * 256, (n + 1) * 256)
        h = [jnp.dot(left[f0], table[f0, :, cols], preferred_element_type=F32) for f0 in range(4)]
        s02, d02, s13, d13 = h[0] + h[2], h[0] - h[2], h[1] + h[3], h[1] - h[3]
        turned = jnp.concatenate([-d13[128:], d13[:128]], axis=0)
        fields = [s02 + s13, d02 + turned, s02 - s13, d02 - turned]
        scaled = []
        for y1 in range(4):
            e = fields[y1].reshape(2, 16, 8, 256)
            power = jnp.sum(e[0] * e[0] + e[1] * e[1], axis=0)
            power = (power + pltpu.roll(power, 4, 0)) * (1.0 / SOURCES)
            intensity[y1 * 4 + n] = jnp.where(upper, power[:, :128], power[:, 128:])
            residual = power - measured[:, y1 * 1024 + n * 256 : y1 * 1024 + (n + 1) * 256]
            scaled.append((e * (residual * GRAD_SCALE)[None, None]).reshape(256, 256))
        s02, d02 = scaled[0] + scaled[2], scaled[0] - scaled[2]
        s13, d13 = scaled[1] + scaled[3], scaled[1] - scaled[3]
        turned = jnp.concatenate([-d13[128:], d13[:128]], axis=0)
        back[0, :, cols] = (s02 + s13).astype(BF16)
        back[1, :, cols] = (d02 - turned).astype(BF16)
        back[2, :, cols] = (s02 - s13).astype(BF16)
        back[3, :, cols] = (d02 + turned).astype(BF16)

    for f0 in range(4):
        both = lax.dot_general(back[f0], table[f0], NT, preferred_element_type=F32)
        for q in range(4):
            cols = slice(q * 128, (q + 1) * 128)
            mixed = sign * both[:128, cols] + pltpu.roll(both[128:, cols], 64, 1)
            parts[q, :, f0 * 128 : (f0 + 1) * 128] = mixed.astype(BF16)
    for q in range(4):
        lined = lax.dot_general(parts[q], order[...], NT, preferred_element_type=F32).astype(BF16)
        for rr in range(4):
            for yl in range(2):
                y[yl * 16 + 4 * q + rr] = lined[yl * 64 : (yl + 1) * 64, rr * 128 : (rr + 1) * 128]


def gradient_kernel(scal, y, table, windows, intensity, out, rows, total):
    rows[...] = y[...].astype(F32).reshape(DEST * 64, 128)
    sign = lane_sign((128, 128))
    total[...] = jnp.zeros_like(total)

    def group(g, carry):
        lefts = []
        for m in range(4):
            u = jnp.concatenate(
                [rows[pl.ds((4 * g + m) * 4 + i, 32, stride=64), :] for i in range(4)], axis=0
            )
            lefts.append(jnp.concatenate([u, sign * pltpu.roll(u, 64, 1)], axis=0).astype(BF16))
        left = jnp.concatenate(lefts, axis=1)
        for n in range(4):
            cols = slice(n * 256, (n + 1) * 256)
            v = lax.dot_general(left, table[:, cols], TN, preferred_element_type=F32)
            real, imag = total[0:64, cols], total[64:128, cols]
            for m in range(4):
                root = scal[2 * g + m // 2, 3 * (m % 2) + 2]
                vr, vi = v[m * 128 : m * 128 + 64], v[m * 128 + 64 : m * 128 + 128]
                w = windows[4 * g + m, :, cols].astype(F32) * root
                wr, wi = w[:64], w[64:]
                real = real + wr * vr + wi * vi
                imag = imag + wr * vi - wi * vr
            total[0:64, cols] = real
            total[64:128, cols] = imag
        return carry

    lax.fori_loop(0, 4, group, 0)
    for t in range(8):
        turned = total[:, t * 128 : (t + 1) * 128].T.astype(BF16)
        for n in range(2):
            out[2 * t + n, 0:64] = turned[n * 64 : (n + 1) * 64]
    power = intensity[...]
    coarse = power.astype(BF16)
    fine = power - coarse.astype(F32)
    out[:, 64:80] = jnp.concatenate([coarse.astype(F32), fine], axis=1).astype(BF16)


def vmem(count):
    return [pl.BlockSpec(memory_space=pltpu.VMEM)] * count


SMEM = pl.BlockSpec(memory_space=pltpu.SMEM)
PARAMS = pltpu.CompilerParams(vmem_limit_bytes=VMEM_LIMIT)


def rows_call(scal, table, here, beyond, pupil):
    return pl.pallas_call(
        rows_kernel,
        out_shape=(
            jax.ShapeDtypeStruct((DEST, 64, 128), BF16),
            jax.ShapeDtypeStruct((16, 128, K), BF16),
        ),
        in_specs=[SMEM] + vmem(4),
        out_specs=tuple(vmem(2)),
        scratch_shapes=[
            pltpu.VMEM((2, K + SH, 128), BF16),
            pltpu.VMEM((2, 256, K + 128), F32),
            pltpu.VMEM((512, K), BF16),
            pltpu.VMEM((DEST * 64, 128), F32),
        ],
        compiler_params=PARAMS,
        name="rows",
    )(scal, table, here, beyond, pupil)


def image_call(x, measured):
    return pl.pallas_call(
        image_kernel,
        out_shape=(
            jax.ShapeDtypeStruct((DEST, 64, 128), BF16),
            jax.ShapeDtypeStruct((16, 8, 128), F32),
        ),
        in_specs=vmem(4),
        out_specs=tuple(vmem(2)),
        scratch_shapes=[
            pltpu.VMEM((4, 256, 512), BF16),
            pltpu.VMEM((4, 256, 1024), BF16),
            pltpu.VMEM((4, 128, 512), BF16),
        ],
        compiler_params=PARAMS,
        name="image",
    )(x, jnp.asarray(lane_order()), jnp.asarray(col_tables()), measured)


def gradient_call(scal, y, table, windows, intensity):
    return pl.pallas_call(
        gradient_kernel,
        out_shape=jax.ShapeDtypeStruct((16, 80, 128), BF16),
        in_specs=[SMEM] + vmem(4),
        out_specs=vmem(1)[0],
        scratch_shapes=[
            pltpu.VMEM((DEST * 64, 128), F32),
            pltpu.VMEM((128, K), F32),
        ],
        compiler_params=PARAMS,
        name="gradient",
    )(scal, y, table, windows, intensity)


def exchange(blocks, axes):
    return lax.all_to_all(blocks, axes, split_axis=0, concat_axis=0, tiled=True)


def shards(pupil, mask_spectrum, shifts, weights, measured):
    z, yl = lax.axis_index("z"), lax.axis_index("yl")
    own = jnp.concatenate([shifts.astype(F32), jnp.sqrt(weights)[:, None]], axis=1).reshape(1, 6)
    scal = exchange(jnp.tile(own, (NZ, 1)), "z")
    beyond = lax.ppermute(mask_spectrum, "row", [(i + 1, i) for i in range(NROW - 1)])
    table = lax.dynamic_index_in_dim(jnp.asarray(row_tables()), z, 0, keepdims=False)
    four = lax.dynamic_slice(measured, (8 * z + 4 * yl, 0), (4, NC))
    four = jnp.concatenate([four, four], axis=0)
    blocks, windows = rows_call(scal, table, mask_spectrum, beyond, pupil.transpose(0, 2, 1))
    blocks, intensity = image_call(exchange(blocks, ("yl", "row")), four)
    blocks = exchange(blocks, ("yl", "row"))
    parts = exchange(gradient_call(scal, blocks, table, windows, intensity), ("z", "yl"))
    grad = jnp.sum(parts[:, :64].astype(F32), axis=0).reshape(64, 2, 64).transpose(1, 0, 2)
    image = (parts[:, 64:72].astype(F32) + parts[:, 72:80].astype(F32)).reshape(16, 2, 4, 128)
    return grad, image.transpose(0, 2, 1, 3).reshape(64, 256)


def solution(mesh):
    finer = Mesh(mesh.devices.reshape(NZ, NYL, NROW), ("z", "yl", "row"))
    src = ("z", "yl")
    return jax.shard_map(
        shards,
        mesh=finer,
        in_specs=(
            P(None, None, "row"),
            P(None, None, "row"),
            P(src, None),
            P(src),
            P("row", None),
        ),
        out_specs=(P(None, src, "row"), P("row", src)),
        check_vma=False,
    )
```

time: 979 us -> 102 us (0.10); the launches traced: 967 us -> 101 us
  matrix products: 505 us -> 0 us
  waiting for transfers between devices: 223 us -> 12.7 us
  local copies, waits for them, and re-layouts: 164 us -> 9.15 us
  blocking collectives: 0 us -> 34.5 us
  Pallas kernels: 0 us -> 24.2 us
  other arithmetic: 24.2 us -> 1.49 us
  between operations: 23.1 us -> 0.7 us
    dot_general x54 -> x0, matrix products: 505 us -> none  [the longest x16 133 us: forward_rows(): jnp.einsum('rf,yf->ry', flat_rows, sine_cols, preferred_element_type=jnp....]
    psum x1 -> x0, waiting for transfers between devices: 143 us -> none  [shards(): summed = lax.psum(partial_image, 'src')]
    unnamed x107 -> x9, local copies, waits for them, and re-layouts: 121 us -> 4.66 us
    unnamed x3 -> x0, waiting for transfers between devices: 68.8 us -> none
    slice x20 -> x0, local copies, waits for them, and re-layouts: 37.5 us -> none  [the longest x16 35.3 us: shards(): back_real = back_real + with_cos[:, 0] + with_sin[:, 1]]
    all_to_all x0 -> x2, blocking collectives: none -> 34.5 us  [exchange(): return lax.all_to_all(blocks, axes, split_axis=0, concat_axis=0, tiled=True)]
    pallas_call x0 -> x3, Pallas kernels: none -> 24.2 us  [the longest x1 9.56 us: rows_call(): pl.pallas_call(rows_kernel, out_shape=(jax.ShapeDtypeStruct((DEST, 64, 12...]
    another operation x5 -> x0, other arithmetic: 18.9 us -> none
  transfers between devices with their start and end apart: 7 -> 3, of which waited for: 4 -> 2; matrix products, arithmetic and copies ran while one was open for 18% -> 8% of each run, Pallas kernels for 0% -> 0%
where the time goes in v1:
time: 102 us; the launch traced here: 101 us
  blocking collectives  34.5 us (34%)
  Pallas kernels  24.2 us (24%)
  starting transfers between devices  18.6 us (18%)
  waiting for transfers between devices  12.7 us (12%)
  local copies, waits for them, and re-layouts  9.15 us (9%)
  other arithmetic  1.49 us (1%)
    all_to_all x2, blocking collectives, exchange(): return lax.all_to_all(blocks, axes, split_axis=0, concat_axis=0, tiled=True)  34.5 us
    all_to_all x2, starting transfers between devices, exchange(): return lax.all_to_all(blocks, axes, split_axis=0, concat_axis=0, tiled=True)  14 us
    all_to_all x2, waiting for transfers between devices, exchange(): return lax.all_to_all(blocks, axes, split_axis=0, concat_axis=0, tiled=True)  12.7 us
    pallas_call x1, Pallas kernels, rows_call(): pl.pallas_call(rows_kernel, out_shape=(jax.ShapeDtypeStruct((DEST, 64, 12...  9.56 us
    pallas_call x1, Pallas kernels, image_call(): pl.pallas_call(image_kernel, out_shape=(jax.ShapeDtypeStruct((DEST, 64, 1...  7.77 us
    pallas_call x1, Pallas kernels, gradient_call(): pl.pallas_call(gradient_kernel, out_shape=jax.ShapeDtypeStruct((16, 80, 1...  6.84 us
    unnamed x9, local copies, waits for them, and re-layouts  4.66 us
    ppermute x1, starting transfers between devices, shards(): lax.ppermute(mask_spectrum, 'row', [(i + 1, i) for i in range(NROW - 1)])  4.65 us
  transfers between devices with their start and end apart: 3, of which 2 were waited for; matrix products, arithmetic and copies ran while one was open for 8% of the time, Pallas kernels for 0%

profile of v1, /device:TPU:2, one launch (start us, length us, event | category | flops | bytes accessed | tf_op | source)
XLA Modules:
  0.0 101.3 jit_solution(6827698541890172007)
XLA Ops:
  0.6 0.0 copy-start
  0.6 4.6 %collective-permute-start = (bf16[2,1088,64]{1,2,0:T(8,128)(2,1)}, bf16[2,1088,64]{1,2,0:T(8,128)(2,1)S(1)}, u32[]{:S(2)}, u32[]{:S(2)}) collective-permute-start(bf16[2,1088,64]{1,2,0:T(8,128)(2,1)} %param.9), channel_id=1, source_target_pairs={{1,0},{2,1},{3,2},{4,3},{5,4},{6,5},{7,6},{8,7},{9,8},{10,9},{11,1... | collective-permute-start | bytes 835592 | tf_op jit(solution)/shard_map/ppermute | solution.py:274
  5.3 0.7 sqrt_bitcast_fusion
  6.0 0.1 copy.19
  6.1 0.7 convert_element_type.12
  6.7 0.1 pad_maximum_fusion.1
  6.8 0.1 tile.8
  6.9 0.6 tile.9
  7.5 8.5 %all-to-all-start = ((f32[8,1,6]{2,1,0:T(1,128)}), f32[8,1,6]{2,1,0:T(1,128)S(1)}, u32[]{:S(2)}, u32[]{:S(2)}) async-start(f32[8,1,6]{2,1,0:T(1,128)} %tile.9), calls=%async_computation | async-start | bytes 8192 | tf_op jit(solution)/shard_map/all_to_all | solution.py:267
  16.0 2.0 %copy.20.here = bf16[2,1088,64]{2,1,0:T(8,128)(2,1)} copy(bf16[2,1088,64]{1,2,0:T(8,128)(2,1)} %param.9) | data formatting | bytes 557056 | tf_op args[1]
  18.0 1.9 %dynamic-slice_bitcast_fusion.table = bf16[256,1024]{1,0:T(8,128)(2,1)} fusion(bf16[8,256,1024]{2,1,0:T(8,128)(2,1)} %constant.32.clone, s32[]{:T(128)S(6)} %select_n.7), kind=kLoop, calls=%fused_computation.1 | loop fusion | bytes 1048580 | tf_op jit(solution)/shard_map/jit(dynamic_index_in_dim)/squeeze | solution.py:275
  19.8 0.0 collective-permute-done
  19.8 1.0 %copy.21.beyond = bf16[2,1088,64]{2,1,0:T(8,128)(2,1)} copy(bf16[2,1088,64]{1,2,0:T(8,128)(2,1)S(1)} %collective-permute-done) | data formatting | bytes 557056 | tf_op jit(solution)/shard_map/ppermute | solution.py:274
  20.9 2.7 %all-to-all-done = f32[8,1,6]{2,1,0:T(1,128)S(1)} async-done(((f32[8,1,6]{2,1,0:T(1,128)}), f32[8,1,6]{2,1,0:T(1,128)S(1)}, u32[]{:S(2)}, u32[]{:S(2)}) %all-to-all-start) | async-done | bytes 224 | tf_op jit(solution)/shard_map/all_to_all | solution.py:267
  23.6 0.0 copy-start.2
  23.6 0.6 copy-done.2
  24.2 9.6 %rows.1 = (bf16[32,64,128]{2,1,0:T(8,128)(2,1)}, bf16[16,128,1024]{2,1,0:T(8,128)(2,1)}) custom-call(f32[8,6]{1,0:T(8,128)} %bitcast.20, bf16[256,1024]{1,0:T(8,128)(2,1)} %dynamic-slice_bitcast_fusion.table, bf16[2,1088,64]{2,1,0:T(8,128)(2,1)} %copy.20.here, bf16[2,1088,64]{2,1,0:T(8,128)(2,1)} %copy.21.beyond, f32[2,64,1024]{2,1,0:T(8,128)} %bitcast.15), custom_call_target="tpu_custom_call" | custom-call | tf_op jit(solution)/shard_map/rows/pallas_call | solution.py:213
  33.7 5.5 %all-to-all-start.1 = ((bf16[32,64,128]{2,1,0:T(8,128)(2,1)}), bf16[32,64,128]{2,1,0:T(8,128)(2,1)S(1)}, u32[]{:S(2)}, u32[]{:S(2)}) async-start(bf16[32,64,128]{2,1,0:T(8,128)(2,1)} %get-tuple-element.6), calls=%async_computation.1 | async-start | bytes 1048576 | tf_op jit(solution)/shard_map/all_to_all | solution.py:267
  39.2 0.0 copy-done
  39.3 0.7 pad_maximum_fusion.measured
  39.9 10.0 %all-to-all-done.1.x = bf16[32,64,128]{2,1,0:T(8,128)(2,1)S(1)} async-done(((bf16[32,64,128]{2,1,0:T(8,128)(2,1)}), bf16[32,64,128]{2,1,0:T(8,128)(2,1)S(1)}, u32[]{:S(2)}, u32[]{:S(2)}) %all-to-all-start.1) | async-done | bytes 524320 | tf_op jit(solution)/shard_map/all_to_all | solution.py:267
  49.9 0.0 copy-start.1
  49.9 0.8 copy-done.1
  50.7 7.8 %image.1 = (bf16[32,64,128]{2,1,0:T(8,128)(2,1)}, f32[16,8,128]{2,1,0:T(8,128)}) custom-call(bf16[32,64,128]{2,1,0:T(8,128)(2,1)} %copy-done.1, bf16[512,512]{1,0:T(8,128)(2,1)} %constant.33.clone.order, bf16[4,512,1024]{2,1,0:T(8,128)(2,1)} %constant.34.clone.table, f32[8,4096]{1,0:T(8,128)} %pad_maximum_fusion.measured), custom_call_target="tpu_custom_call" | custom-call | tf_op jit(solution)/shard_map/image/pallas_call | solution.py:233
  58.5 16.4 %all_to_all.23.y = bf16[32,64,128]{2,1,0:T(8,128)(2,1)} all-to-all(bf16[32,64,128]{2,1,0:T(8,128)(2,1)} %get-tuple-element.7), channel_id=1, replica_groups=mesh['z'=8,'yl'=2,'row'=16] {'yl','row'}, dimensions={0} | all-to-all | bytes 1048576 | tf_op jit(solution)/shard_map/all_to_all | solution.py:267
  74.9 6.8 %gradient.1 = bf16[16,80,128]{2,1,0:T(8,128)(2,1)} custom-call(f32[8,6]{1,0:T(8,128)} %bitcast.21, bf16[32,64,128]{2,1,0:T(8,128)(2,1)} %all_to_all.23.y, bf16[256,1024]{1,0:T(8,128)(2,1)} %dynamic-slice_bitcast_fusion.table, bf16[16,128,1024]{2,1,0:T(8,128)(2,1)} %get-tuple-element.8.windows, f32[16,8,128]{2,1,0:T(8,128)} %get-tuple-element.9.intensity), custom_call_target="tpu_custom_call" | custom-call | tf_op jit(solution)/shard_map/gradient/pallas_call | solution.py:252
  81.7 18.1 %all_to_all.24 = bf16[16,80,128]{2,1,0:T(8,128)(2,1)S(1)} all-to-all(bf16[16,80,128]{2,1,0:T(8,128)(2,1)} %gradient.1), channel_id=1, replica_groups=mesh['z'=8,'yl'=2,'row'=16] {'z','yl'}, dimensions={0} | all-to-all | bytes 655360 | tf_op jit(solution)/shard_map/all_to_all | solution.py:267
  99.9 0.1 reshape.23
  100.0 0.6 copy.23
  100.7 0.6 copy.26
  (4 shorter events, 0.1 us)
Async XLA Ops:
  0.6 38.6 %copy-start = (f32[64,4096]{1,0:T(8,128)S(1)}, f32[64,4096]{1,0:T(8,128)}, u32[]{:S(2)}) copy-start(f32[64,4096]{1,0:T(8,128)} %param.12) | copy-start | bytes 3145732
  0.6 19.2 %collective-permute-start = (bf16[2,1088,64]{1,2,0:T(8,128)(2,1)}, bf16[2,1088,64]{1,2,0:T(8,128)(2,1)S(1)}, u32[]{:S(2)}, u32[]{:S(2)}) collective-permute-start(bf16[2,1088,64]{1,2,0:T(8,128)(2,1)} %param.9), channel_id=1, source_target_pairs={{1,0},{2,1},{3,2},{4,3},{5,4},{6,5},{7,6},{8,7},{9,8},{10,9},{11,1... | collective-permute-start | bytes 835592 | tf_op jit(solution)/shard_map/ppermute | solution.py:274
  7.5 16.1 %all-to-all-start = ((f32[8,1,6]{2,1,0:T(1,128)}), f32[8,1,6]{2,1,0:T(1,128)S(1)}, u32[]{:S(2)}, u32[]{:S(2)}) async-start(f32[8,1,6]{2,1,0:T(1,128)} %tile.9), calls=%async_computation | async-start | bytes 8192 | tf_op jit(solution)/shard_map/all_to_all | solution.py:267
  23.6 0.6 copy-start.2
  33.7 16.2 %all-to-all-start.1 = ((bf16[32,64,128]{2,1,0:T(8,128)(2,1)}), bf16[32,64,128]{2,1,0:T(8,128)(2,1)S(1)}, u32[]{:S(2)}, u32[]{:S(2)}) async-start(bf16[32,64,128]{2,1,0:T(8,128)(2,1)} %get-tuple-element.6), calls=%async_computation.1 | async-start | bytes 1048576 | tf_op jit(solution)/shard_map/all_to_all | solution.py:267
  49.9 0.8 copy-start.1

commit v2 on v1

v2 whole, which is shorter than its diff:
```python
import functools
import math

import jax
import jax.numpy as jnp
import ml_dtypes
import numpy as np
from jax import lax
from jax.experimental import pallas as pl
from jax.experimental.pallas import tpu as pltpu
from jax.sharding import Mesh, PartitionSpec as P

K = 1024
NC = 4096
NR = 1024
SOURCES = 32
SH = 64
NZ = 8
NYL = 2
NROW = 16
DEST = NYL * NROW
GRAD_SCALE = 2.0 / math.sqrt(SOURCES * NR * NC)
VMEM_LIMIT = 20 * 1024 * 1024
F32 = jnp.float32
BF16 = jnp.bfloat16
NT = (((1,), (1,)), ((), ()))
TN = (((0,), (0,)), ((), ()))


def phase(position, frequency):
    turns = np.mod(position * frequency, NC).astype(np.float32)
    angle = turns * np.float32(2.0 * math.pi / NC)
    return np.cos(angle), np.sin(angle)


@functools.cache
def row_tables():
    z, yl, row, i = np.meshgrid(np.arange(NZ), np.arange(NYL), np.arange(NROW), np.arange(4), indexing="ij")
    x = (64 * row + 8 * z + 4 * yl + i).reshape(NZ, 128, 1)
    cosine, sine = phase(x, np.arange(K) - K // 2)
    return np.concatenate([cosine, sine], axis=1).astype(ml_dtypes.bfloat16)


@functools.cache
def col_tables():
    f0, q, rr, k1 = np.meshgrid(np.arange(4), np.arange(4), np.arange(4), np.arange(16), indexing="ij")
    f = (64 * (4 * q + rr) + 4 * k1 + f0 - K // 2).reshape(4, 4, 64, 1)
    cosine, sine = phase(f, np.arange(1024))
    return np.stack([cosine, sine], axis=2).reshape(4, 512, 1024).astype(ml_dtypes.bfloat16)


@functools.cache
def lane_order():
    rr, c, k = np.meshgrid(np.arange(4), np.arange(2), np.arange(64), indexing="ij")
    target = (k % 4) * 128 + c * 64 + rr * 16 + k // 4
    order = np.zeros((512, 512), np.float32)
    order[np.arange(512), target.reshape(-1)] = 1.0
    return order.astype(ml_dtypes.bfloat16)


def lane_sign(shape):
    lane = lax.broadcasted_iota(jnp.int32, shape, len(shape) - 1)
    return jnp.where((lane & 127) < 64, 1.0, -1.0).astype(F32)


def root_columns(low, high):
    lane = lax.broadcasted_iota(jnp.int32, (128, 128), 1)
    return jnp.where((lane & 32) == 0, low, high)


def swap_rows(a, b):
    low = lax.broadcasted_iota(jnp.int32, a.shape, 1) < 4
    return jnp.where(low, a, pltpu.roll(b, 4, 1)), jnp.where(low, pltpu.roll(a, 4, 1), b)


def stage_kernel(place, here, pupil, measured, mask, share, four, eight, arrived):
    rows = pl.ds(pl.multiple_of(place[0] * 8, 8), 8)
    copy = pltpu.make_async_copy(measured.at[rows, :], eight, arrived)
    copy.start()
    first = pl.multiple_of(place[1] * 32, 32)
    for c in range(2):
        for t in range(9):
            width = 128 if t < 8 else SH
            mask[c, t, :, :width] = here[c, :, t * 128 : t * 128 + width].astype(F32)
        for t in range(8):
            share[c, t] = pupil[c, pl.ds(first, 32), t * 128 : (t + 1) * 128]
    copy.wait()
    upper = lax.broadcasted_iota(jnp.int32, (8, NC), 0) >= 4
    wanted = upper == (place[1] == 1)
    four[...] = jnp.where(wanted, eight[...], pltpu.roll(eight[...], 4, 0))


def rows_kernel(
    gathered, table, here, beyond, share, far, out, windows, roots, near, scal, mask, fields, arrived, loaded
):
    copy = pltpu.make_async_copy(gathered, scal, arrived)
    copy.start()
    load = pltpu.make_async_copy(far, near, loaded)
    load.start()
    for c in range(2):
        for t in range(9):
            width = 128 if t < 8 else SH
            mask[c, t, 0:64, :width] = here[c, t, :, :width]
            mask[c, t, 64:128, :width] = beyond[c, :, t * 128 : t * 128 + width].astype(F32)
    copy.wait()
    for m in range(2):
        for p in range(16):
            at = m * 64 + p * 4
            roots[at : at + 4, :] = jnp.full((4, 128), scal[p, 0, 3 * m + 2])
    lane = lax.broadcasted_iota(jnp.int32, (32, 128), 1)
    sign = -lane_sign((128, 128))

    def build(p, field, at):
        first = [scal[p, 0, 3 * m + 1].astype(jnp.int32) for m in range(2)]
        by = [scal[p, 0, 3 * m].astype(jnp.int32) for m in range(2)]
        turn = [(128 - a) & 127 for a in by]
        keep = [lane < 128 - a for a in by]

        def turned(c, t, m):
            return pltpu.roll(mask[c, t, pl.ds(first[m], 32), :], turn[m], 1)

        before = [[turned(c, 0, m) for c in range(2)] for m in range(2)]
        for t in range(8):
            cols = slice(t * 128, (t + 1) * 128)
            pr, pi = share[0, t], share[1, t]
            for m in range(2):
                after = [turned(c, t + 1, m) for c in range(2)]
                wr, wi = [jnp.where(keep[m], before[m][c], after[c]) for c in range(2)]
                before[m] = after
                low, high = m * 32, 64 + m * 32
                field[at + low : at + low + 32, cols] = (pr * wr - pi * wi).astype(BF16)
                field[at + high : at + high + 32, cols] = (pr * wi + pi * wr).astype(BF16)
                windows[p, low : low + 32, cols] = wr.astype(BF16)
                windows[p, high : high + 32, cols] = wi.astype(BF16)

    def transform(g, field):
        mixed = []
        for half in range(2):
            rows = field[half * 256 : (half + 1) * 256, :]
            both = lax.dot_general(table[...], rows, NT, preferred_element_type=F32)
            for n in range(2):
                p = 4 * g + 2 * half + n
                by_cos = both[:128, n * 128 : (n + 1) * 128]
                by_sin = both[128:, n * 128 : (n + 1) * 128]
                root = root_columns(scal[p, 0, 2], scal[p, 0, 5]) * (1.0 / K)
                mixed.append(((by_cos + sign * pltpu.roll(by_sin, 64, 1)) * root).reshape(16, 8, 128))
        first, second = swap_rows(mixed[0], mixed[1]), swap_rows(mixed[2], mixed[3])
        for n in range(2):
            tile = jnp.concatenate([first[n], second[n]], axis=1).astype(BF16)
            out[:, n, g * 16 : (g + 1) * 16, :] = tile

    for g in range(5):
        if g < 4:
            for n in range(4):
                build(4 * g + n, fields.at[g], n * 128)
        if g > 0:
            transform(g - 1, fields.at[g - 1])
    load.wait()


def swap_halves(a, b):
    low = (lax.broadcasted_iota(jnp.int32, a.shape, 1) & 32) == 0
    return jnp.where(low, a, pltpu.roll(b, 32, 1)), jnp.where(low, pltpu.roll(a, 96, 1), b)


def image_kernel(x, order, table, measured, roots, y, intensity, left, back, parts):
    sign = lane_sign((128, 128))
    for q in range(4):
        tiles = []
        for rr in range(4):
            r = 4 * q + rr
            tiles.append(jnp.concatenate(swap_halves(x[r].astype(F32), x[16 + r].astype(F32)), axis=0))
        lined = jnp.concatenate(tiles, axis=1).astype(BF16)
        sorted_lanes = jnp.dot(lined, order[...], preferred_element_type=F32)
        for f0 in range(4):
            tile = sorted_lanes[:, f0 * 128 : (f0 + 1) * 128]
            left[f0, 0:128, q * 128 : (q + 1) * 128] = (tile * sign).astype(BF16)
            left[f0, 128:256, q * 128 : (q + 1) * 128] = pltpu.roll(tile, 64, 1).astype(BF16)

    upper = lax.broadcasted_iota(jnp.int32, (8, 128), 0) < 4
    for n in range(4):
        cols = slice(n * 256, (n + 1) * 256)
        h = [jnp.dot(left[f0], table[f0, :, cols], preferred_element_type=F32) for f0 in range(4)]
        s02, d02, s13, d13 = h[0] + h[2], h[0] - h[2], h[1] + h[3], h[1] - h[3]
        turned = jnp.concatenate([-d13[128:], d13[:128]], axis=0)
        fields = [s02 + s13, d02 + turned, s02 - s13, d02 - turned]
        scaled = []
        for y1 in range(4):
            e = fields[y1].reshape(2, 16, 8, 256)
            power = jnp.sum(e[0] * e[0] + e[1] * e[1], axis=0)
            power = (power + pltpu.roll(power, 4, 0)) * (1.0 / SOURCES)
            intensity[y1 * 4 + n] = jnp.where(upper, power[:, :128], power[:, 128:])
            residual = power - measured[:, y1 * 1024 + n * 256 : y1 * 1024 + (n + 1) * 256]
            scaled.append((e * (residual * GRAD_SCALE)[None, None]).reshape(256, 256))
        s02, d02 = scaled[0] + scaled[2], scaled[0] - scaled[2]
        s13, d13 = scaled[1] + scaled[3], scaled[1] - scaled[3]
        turned = jnp.concatenate([-d13[128:], d13[:128]], axis=0)
        back[0, :, cols] = (s02 + s13).astype(BF16)
        back[1, :, cols] = (d02 - turned).astype(BF16)
        back[2, :, cols] = (s02 - s13).astype(BF16)
        back[3, :, cols] = (d02 + turned).astype(BF16)

    for f0 in range(4):
        both = lax.dot_general(back[f0], table[f0], NT, preferred_element_type=F32)
        for q in range(4):
            cols = slice(q * 128, (q + 1) * 128)
            mixed = sign * both[:128, cols] + pltpu.roll(both[128:, cols], 64, 1)
            parts[q, :, f0 * 128 : (f0 + 1) * 128] = (mixed * roots[...]).astype(BF16)
    for q in range(4):
        lined = lax.dot_general(parts[q], order[...], NT, preferred_element_type=F32)
        for rr in range(4):
            tile = lined[:, rr * 128 : (rr + 1) * 128]
            low, high = swap_halves(tile[:64], tile[64:])
            y[4 * q + rr] = low.astype(BF16)
            y[16 + 4 * q + rr] = high.astype(BF16)


def gradient_kernel(y, table, windows, intensity, out, total):
    sign = lane_sign((128, 128))
    total[...] = jnp.zeros_like(total)

    def group(g, carry):
        tiles = [y[:, n, pl.ds(pl.multiple_of(g * 16, 16), 16), :].astype(F32) for n in range(2)]
        lefts = []
        for half in range(2):
            part = slice(half * 8, (half + 1) * 8)
            for u in swap_rows(tiles[0][:, part], tiles[1][:, part]):
                u = u.reshape(128, 128)
                lefts.append(jnp.concatenate([u, sign * pltpu.roll(u, 64, 1)], axis=0).astype(BF16))
        left = jnp.concatenate(lefts, axis=1)
        for n in range(4):
            cols = slice(n * 256, (n + 1) * 256)
            v = lax.dot_general(left, table[:, cols], TN, preferred_element_type=F32)
            real, imag = total[0:64, cols], total[64:128, cols]
            for m in range(4):
                vr, vi = v[m * 128 : m * 128 + 64], v[m * 128 + 64 : m * 128 + 128]
                w = windows[4 * g + m, :, cols].astype(F32)
                wr, wi = w[:64], w[64:]
                real = real + wr * vr + wi * vi
                imag = imag + wr * vi - wi * vr
            total[0:64, cols] = real
            total[64:128, cols] = imag
        return carry

    lax.fori_loop(0, 4, group, 0)
    for t in range(8):
        cols = slice(t * 128, (t + 1) * 128)
        real = total[0:32, cols] + total[32:64, cols]
        imag = total[64:96, cols] + total[96:128, cols]
        turned = jnp.concatenate([real, imag], axis=0).T
        for n in range(2):
            both = jnp.concatenate([turned[n * 64 : n * 64 + 32], turned[n * 64 + 32 : n * 64 + 64]], axis=1)
            out[2 * t + n, 0:32] = both.astype(BF16)
    power = intensity[...]
    coarse = power.astype(BF16).astype(F32)
    out[:, 32:48] = jnp.concatenate([coarse, power - coarse], axis=1).astype(BF16)


def final_kernel(parts, grad, image):
    for yl in range(2):
        total = jnp.sum(
            jnp.stack([parts[2 * z + yl, 0:32].astype(F32) for z in range(NZ)]), axis=0
        )
        for h in range(2):
            for c in range(2):
                start = h * 64 + c * 32
                grad[c, h * 32 : (h + 1) * 32, yl * 32 : (yl + 1) * 32] = total[:, start : start + 32]
    for j in range(16):
        both = parts[j, 32:48].astype(F32)
        power = both[:8] + both[8:]
        for h in range(2):
            image[4 * j : 4 * j + 4, h * 128 : (h + 1) * 128] = power[4 * h : 4 * h + 4]


def vmem(count):
    return [pl.BlockSpec(memory_space=pltpu.VMEM)] * count


HBM = pl.BlockSpec(memory_space=pltpu.HBM)
ANY = pl.BlockSpec(memory_space=pl.ANY)
SMEM = pl.BlockSpec(memory_space=pltpu.SMEM)
SMALL = pltpu.CompilerParams(vmem_limit_bytes=6 * 1024 * 1024)
PARAMS = pltpu.CompilerParams(vmem_limit_bytes=VMEM_LIMIT)


def kept(array):
    return pltpu.with_memory_space_constraint(array, pltpu.VMEM)


def own_kernel(shifts, weights, out):
    place = lax.broadcasted_iota(jnp.int32, (16, 128), 1)
    column = ((lax.broadcasted_iota(jnp.int32, (16, 128), 0) & 1) * 32).astype(F32)
    own = column
    for m in range(2):
        own = jnp.where(place == 3 * m, shifts[m, 0].astype(F32), own)
        own = jnp.where(place == 3 * m + 1, shifts[m, 1].astype(F32) + column, own)
        own = jnp.where(place == 3 * m + 2, jnp.sqrt(jnp.full((16, 128), weights[m])), own)
    out[:, 0, :] = own


def own_call(shifts, weights):
    return pl.pallas_call(
        own_kernel,
        out_shape=jax.ShapeDtypeStruct((16, 1, 128), F32),
        in_specs=[SMEM, SMEM],
        out_specs=vmem(1)[0],
        name="own",
    )(shifts, weights)


def stage_call(place, here, pupil, measured):
    return pl.pallas_call(
        stage_kernel,
        out_shape=(
            pltpu.VMEM((2, 9, 64, 128), F32),
            pltpu.VMEM((2, 8, 32, 128), F32),
            pltpu.VMEM((8, NC), F32),
        ),
        in_specs=[SMEM] + vmem(2) + [HBM],
        out_specs=tuple(vmem(3)),
        scratch_shapes=[pltpu.VMEM((8, NC), F32), pltpu.SemaphoreType.DMA],
        compiler_params=SMALL,
        name="stage",
    )(place, here, pupil, pltpu.with_memory_space_constraint(measured, pltpu.HBM))


def rows_call(scal, table, here, beyond, share):
    far = pltpu.with_memory_space_constraint(jnp.asarray(col_tables()), pltpu.HBM)
    return pl.pallas_call(
        rows_kernel,
        out_shape=(
            jax.ShapeDtypeStruct((16, 2, 64, 128), BF16),
            pltpu.VMEM((16, 128, K), BF16),
            pltpu.VMEM((128, 128), F32),
            pltpu.VMEM((4, 512, 1024), BF16),
        ),
        in_specs=[ANY] + vmem(4) + [HBM],
        out_specs=tuple(vmem(4)),
        scratch_shapes=[
            pltpu.SMEM((16, 1, 128), F32),
            pltpu.VMEM((2, 9, 128, 128), F32),
            pltpu.VMEM((4, 512, K), BF16),
            pltpu.SemaphoreType.DMA,
            pltpu.SemaphoreType.DMA,
        ],
        compiler_params=PARAMS,
        name="rows",
    )(scal, kept(table), kept(here), kept(beyond), kept(share), far)


def image_call(x, table, measured, roots):
    return pl.pallas_call(
        image_kernel,
        out_shape=(
            jax.ShapeDtypeStruct((DEST, 64, 128), BF16),
            pltpu.VMEM((16, 8, 128), F32),
        ),
        in_specs=vmem(5),
        out_specs=tuple(vmem(2)),
        scratch_shapes=[
            pltpu.VMEM((4, 256, 512), BF16),
            pltpu.VMEM((4, 256, 1024), BF16),
            pltpu.VMEM((4, 128, 512), BF16),
        ],
        compiler_params=PARAMS,
        name="image",
    )(x, kept(jnp.asarray(lane_order())), kept(table), kept(measured), kept(roots))


def gradient_call(y, table, windows, intensity):
    return pl.pallas_call(
        gradient_kernel,
        out_shape=jax.ShapeDtypeStruct((16, 48, 128), BF16),
        in_specs=vmem(4),
        out_specs=vmem(1)[0],
        scratch_shapes=[pltpu.VMEM((128, K), F32)],
        compiler_params=PARAMS,
        name="gradient",
    )(y.reshape(16, 2, 64, 128), kept(table), kept(windows), kept(intensity))


def final_call(parts):
    return pl.pallas_call(
        final_kernel,
        out_shape=(jax.ShapeDtypeStruct((2, 64, 64), F32), jax.ShapeDtypeStruct((64, 256), F32)),
        in_specs=vmem(1),
        out_specs=tuple(vmem(2)),
        compiler_params=SMALL,
        name="final",
    )(kept(parts))


def exchange(blocks, axes):
    return lax.all_to_all(blocks, axes, split_axis=0, concat_axis=0, tiled=True)


def shards(pupil, mask_spectrum, shifts, weights, measured):
    z, yl = lax.axis_index("z"), lax.axis_index("yl")
    mask = mask_spectrum.transpose(0, 2, 1)
    own, late = lax.optimization_barrier((own_call(shifts, weights), mask))
    scal = exchange(own, ("z", "yl"))
    beyond = lax.ppermute(late, "row", [(i + 1, i) for i in range(NROW - 1)])
    place = jnp.stack([z, yl]).astype(jnp.int32)
    here, share, four = stage_call(place, mask, pupil.transpose(0, 2, 1), measured)
    table = lax.dynamic_index_in_dim(jnp.asarray(row_tables()), z, 0, keepdims=False)
    blocks, windows, roots, near = rows_call(scal, table, here, beyond, share)
    blocks, intensity = image_call(exchange(blocks.reshape(DEST, 64, 128), ("yl", "row")), near, four, roots)
    blocks = exchange(blocks, ("yl", "row"))
    parts = exchange(gradient_call(blocks, table, windows, intensity), ("z", "yl"))
    return final_call(parts)


def solution(mesh):
    finer = Mesh(mesh.devices.reshape(NZ, NYL, NROW), ("z", "yl", "row"))
    src = ("z", "yl")
    return jax.shard_map(
        shards,
        mesh=finer,
        in_specs=(
            P(None, None, "row"),
            P(None, None, "row"),
            P(src, None),
            P(src),
            P("row", None),
        ),
        out_specs=(P(None, src, "row"), P("row", src)),
        check_vma=False,
    )
```

time: 102 us -> 83.6 us (0.82)
  blocking collectives: 34.5 us -> 46.3 us
  waiting for transfers between devices: 12.7 us -> 3.77 us
  Pallas kernels: 24.2 us -> 16 us
  local copies, waits for them, and re-layouts: 9.15 us -> 3.09 us
  starting transfers between devices: 18.6 us -> 13.2 us
  other arithmetic: 1.49 us -> 0.08 us
    all_to_all x2 -> x3, blocking collectives: 34.5 us -> 46.3 us  [exchange(): return lax.all_to_all(blocks, axes, split_axis=0, concat_axis=0, tiled=True)]
    all_to_all x2 -> x1, waiting for transfers between devices: 12.7 us -> 3.77 us  [exchange(): return lax.all_to_all(blocks, axes, split_axis=0, concat_axis=0, tiled=True)]
    all_to_all x2 -> x1, starting transfers between devices: 14 us -> 8.7 us  [exchange(): return lax.all_to_all(blocks, axes, split_axis=0, concat_axis=0, tiled=True)]
    pallas_call x2 -> x5, Pallas kernels: 16.4 us -> 11.4 us  [the longest x1 4.46 us: rows_call(): pl.pallas_call(rows_kernel, out_shape=(jax.ShapeDtypeStruct((16, 2, 64, 1...]
    pallas_call x1, Pallas kernels: 7.77 us -> 4.57 us  [image_call(): pl.pallas_call(image_kernel, out_shape=(jax.ShapeDtypeStruct((DEST, 64, 1...]
    unnamed x9 -> x6, local copies, waits for them, and re-layouts: 4.66 us -> 2.01 us
    ppermute x1 -> x0, local copies, waits for them, and re-layouts: 1.03 us -> none  [shards(): lax.ppermute(mask_spectrum, 'row', [(i + 1, i) for i in range(NROW - 1)])]
  transfers between devices with their start and end apart: 3 -> 2, of which waited for: 2 -> 1; matrix products, arithmetic and copies ran while one was open for 8% -> 1% of each run, Pallas kernels for 0% -> 2%
where the time goes in v2:
time: 83.6 us; the launch traced here: 83.2 us
  blocking collectives  46.3 us (55%)
  Pallas kernels  16 us (19%)
  starting transfers between devices  13.2 us (16%)
  waiting for transfers between devices  3.77 us (5%)
  local copies, waits for them, and re-layouts  3.09 us (4%)
    all_to_all x3, blocking collectives, exchange(): return lax.all_to_all(blocks, axes, split_axis=0, concat_axis=0, tiled=True)  46.3 us
    all_to_all x1, starting transfers between devices, exchange(): return lax.all_to_all(blocks, axes, split_axis=0, concat_axis=0, tiled=True)  8.7 us
    pallas_call x1, Pallas kernels, image_call(): pl.pallas_call(image_kernel, out_shape=(jax.ShapeDtypeStruct((DEST, 64, 1...  4.57 us
    ppermute x1, starting transfers between devices, shards(): beyond = lax.ppermute(late, 'row', [(i + 1, i) for i in range(NROW - 1)])  4.5 us
    pallas_call x1, Pallas kernels, rows_call(): pl.pallas_call(rows_kernel, out_shape=(jax.ShapeDtypeStruct((16, 2, 64, 1...  4.46 us
    all_to_all x1, waiting for transfers between devices, exchange(): return lax.all_to_all(blocks, axes, split_axis=0, concat_axis=0, tiled=True)  3.77 us
    pallas_call x1, Pallas kernels, gradient_call(): pl.pallas_call(gradient_kernel, out_shape=jax.ShapeDtypeStruct((16, 48, 1...  3.47 us
    unnamed x6, local copies, waits for them, and re-layouts  2.01 us
  transfers between devices with their start and end apart: 2, of which 1 were waited for; matrix products, arithmetic and copies ran while one was open for 1% of the time, Pallas kernels for 2%

profile of v2, /device:TPU:2, one launch (start us, length us, event | category | flops | bytes accessed | tf_op | source)
XLA Modules:
  0.0 83.2 jit_solution(14074584086412284965)
XLA Ops:
  0.6 1.3 %own.1 = f32[16,1,128]{2,1,0:T(1,128)} custom-call(s32[2,2]{1,0:T(2,128)} %shifts.1, f32[2]{0:T(128)} %weights.1), custom_call_target="tpu_custom_call" | custom-call | tf_op jit(solution)/shard_map/own/pallas_call | solution.py:302
  1.9 4.5 %collective-permute-start = (bf16[2,64,1088]{2,1,0:T(8,128)(2,1)}, bf16[2,64,1088]{2,1,0:T(8,128)(2,1)S(1)}, u32[]{:S(2)}, u32[]{:S(2)}) collective-permute-start(bf16[2,64,1088]{2,1,0:T(8,128)(2,1)} %bitcast.11), channel_id=1, source_target_pairs={{1,0},{2,1},{3,2},{4,3},{5,4},{6,5},{7,6},{8,7},{9,8},{10,9},{11,1... | collective-permute-start | bytes 835592 | tf_op jit(solution)/shard_map/ppermute | solution.py:402
  6.4 8.7 %all-to-all-start = ((f32[16,1,128]{2,1,0:T(1,128)}), f32[16,1,128]{2,1,0:T(1,128)S(1)}, u32[]{:S(2)}, u32[]{:S(2)}) async-start(f32[16,1,128]{2,1,0:T(1,128)} %own.1), calls=%async_computation | async-start | bytes 16384 | tf_op jit(solution)/shard_map/all_to_all | solution.py:394
  15.2 1.1 %dynamic-slice_bitcast_fusion.table = bf16[256,1024]{1,0:T(8,128)(2,1)S(1)} fusion(bf16[8,256,1024]{2,1,0:T(8,128)(2,1)} %constant.24.clone, s32[]{:T(128)S(6)} %select_n.4), kind=kLoop, calls=%fused_computation | loop fusion | bytes 1048580 | tf_op jit(solution)/shard_map/jit(dynamic_index_in_dim)/squeeze | solution.py:405
  16.2 0.1 pad_add_fusion.place
  16.3 0.0 copy-start
  16.3 1.0 %copy-done = f32[2,1024,64]{1,2,0:T(8,128)S(1)} copy-done((f32[2,1024,64]{1,2,0:T(8,128)S(1)}, f32[2,1024,64]{1,2,0:T(8,128)}, u32[]{:S(2)}) %copy-start) | copy-done | bytes 524312
  17.4 0.0 copy-start.2
  17.4 1.0 %copy-done.2 = bf16[2,1088,64]{1,2,0:T(8,128)(2,1)S(1)} copy-done((bf16[2,1088,64]{1,2,0:T(8,128)(2,1)S(1)}, bf16[2,1088,64]{1,2,0:T(8,128)(2,1)}, u32[]{:S(2)}) %copy-start.2) | copy-done | bytes 278552
  18.3 0.0 copy-start.1
  18.3 1.5 %stage.1 = (f32[2,9,64,128]{3,2,1,0:T(8,128)S(1)}, f32[2,8,32,128]{3,2,1,0:T(8,128)S(1)}, f32[8,4096]{1,0:T(8,128)S(1)}) custom-call(s32[2]{0:T(128)S(1)} %pad_add_fusion.place, bf16[2,64,1088]{2,1,0:T(8,128)(2,1)S(1)} %bitcast.12, f32[2,64,1024]{2,1,0:T(8,128)S(1)} %bitcast.10, f32[64,4096]{1,0:T(8,128)} %measured.1), custom_call_target="tpu_custom_call" | custom-call | tf_op jit(solution)/shard_map/stage/pallas_call | solution.py:312
  19.8 3.8 %all-to-all-done.gathered = f32[16,1,128]{2,1,0:T(1,128)S(1)} async-done(((f32[16,1,128]{2,1,0:T(1,128)}), f32[16,1,128]{2,1,0:T(1,128)S(1)}, u32[]{:S(2)}, u32[]{:S(2)}) %all-to-all-start) | async-done | bytes 8224 | tf_op jit(solution)/shard_map/all_to_all | solution.py:394
  23.6 0.0 collective-permute-done.beyond
  23.6 4.5 %rows.1 = (bf16[16,2,64,128]{3,2,1,0:T(8,128)(2,1)S(1)}, bf16[16,128,1024]{2,1,0:T(8,128)(2,1)S(1)}, f32[128,128]{1,0:T(8,128)S(1)}, bf16[4,512,1024]{2,1,0:T(8,128)(2,1)S(1)}) custom-call(f32[16,1,128]{2,1,0:T(1,128)S(1)} %all-to-all-done.gathered, bf16[256,1024]{1,0:T(8,128)(2,1)S(1)} %dynamic-slice_bitcast_fusion.table, ...), custom_call_target="tpu_custom_call" | custom-call | tf_op jit(solution)/shard_map/rows/pallas_call | solution.py:329
  28.0 16.8 %all_to_all.20.x = bf16[32,64,128]{2,1,0:T(8,128)(2,1)S(1)} all-to-all(bf16[32,64,128]{2,1,0:T(8,128)(2,1)S(1)} %bitcast.9), channel_id=1, replica_groups=mesh['z'=8,'yl'=2,'row'=16] {'yl','row'}, dimensions={0} | all-to-all | bytes 1048576 | tf_op jit(solution)/shard_map/all_to_all | solution.py:394
  44.9 0.0 copy-done.1
  44.9 4.6 %image.1 = (bf16[32,64,128]{2,1,0:T(8,128)(2,1)S(1)}, f32[16,8,128]{2,1,0:T(8,128)S(1)}) custom-call(bf16[32,64,128]{2,1,0:T(8,128)(2,1)S(1)} %all_to_all.20.x, bf16[512,512]{1,0:T(8,128)(2,1)S(1)} %copy-done.1, bf16[4,512,1024]{2,1,0:T(8,128)(2,1)S(1)} %get-tuple-element.18.table, f32[8,4096]{1,0:T(8,128)S(1)} %get-tuple-element.19.measured, ...), custom_call_target="tpu_custom_call" | custom-call | tf_op jit(solution)/shard_map/image/pallas_call | solution.py:352
  49.4 15.1 %all_to_all.21 = bf16[32,64,128]{2,1,0:T(8,128)(2,1)S(1)} all-to-all(bf16[32,64,128]{2,1,0:T(8,128)(2,1)S(1)} %get-tuple-element.21), channel_id=1, replica_groups=mesh['z'=8,'yl'=2,'row'=16] {'yl','row'}, dimensions={0} | all-to-all | bytes 1048576 | tf_op jit(solution)/shard_map/all_to_all | solution.py:394
  64.6 3.5 %gradient.1 = bf16[16,48,128]{2,1,0:T(8,128)(2,1)S(1)} custom-call(bf16[16,2,64,128]{3,2,1,0:T(8,128)(2,1)S(1)} %bitcast.8, bf16[256,1024]{1,0:T(8,128)(2,1)S(1)} %dynamic-slice_bitcast_fusion.table, bf16[16,128,1024]{2,1,0:T(8,128)(2,1)S(1)} %get-tuple-element.22.windows, f32[16,8,128]{2,1,0:T(8,128)S(1)} %get-tuple-element.23.intensity), custom_call_target="tpu_custom_call" | custom-call | tf_op jit(solution)/shard_map/gradient/pallas_call | solution.py:371
  68.0 14.4 %all_to_all.22.parts = bf16[16,48,128]{2,1,0:T(8,128)(2,1)S(1)} all-to-all(bf16[16,48,128]{2,1,0:T(8,128)(2,1)S(1)} %gradient.1), channel_id=1, replica_groups=mesh['z'=8,'yl'=2,'row'=16] {'z','yl'}, dimensions={0} | all-to-all | bytes 393216 | tf_op jit(solution)/shard_map/all_to_all | solution.py:394
  82.4 0.7 final.1
Async XLA Ops:
  1.9 21.6 %collective-permute-start = (bf16[2,64,1088]{2,1,0:T(8,128)(2,1)}, bf16[2,64,1088]{2,1,0:T(8,128)(2,1)S(1)}, u32[]{:S(2)}, u32[]{:S(2)}) collective-permute-start(bf16[2,64,1088]{2,1,0:T(8,128)(2,1)} %bitcast.11), channel_id=1, source_target_pairs={{1,0},{2,1},{3,2},{4,3},{5,4},{6,5},{7,6},{8,7},{9,8},{10,9},{11,1... | collective-permute-start | bytes 835592 | tf_op jit(solution)/shard_map/ppermute | solution.py:402
  6.4 17.1 %all-to-all-start = ((f32[16,1,128]{2,1,0:T(1,128)}), f32[16,1,128]{2,1,0:T(1,128)S(1)}, u32[]{:S(2)}, u32[]{:S(2)}) async-start(f32[16,1,128]{2,1,0:T(1,128)} %own.1), calls=%async_computation | async-start | bytes 16384 | tf_op jit(solution)/shard_map/all_to_all | solution.py:394
  16.3 1.0 %copy-start = (f32[2,1024,64]{1,2,0:T(8,128)S(1)}, f32[2,1024,64]{1,2,0:T(8,128)}, u32[]{:S(2)}) copy-start(f32[2,1024,64]{1,2,0:T(8,128)} %param.8) | copy-start | bytes 1572868
  17.4 1.0 %copy-start.2 = (bf16[2,1088,64]{1,2,0:T(8,128)(2,1)S(1)}, bf16[2,1088,64]{1,2,0:T(8,128)(2,1)}, u32[]{:S(2)}) copy-start(bf16[2,1088,64]{1,2,0:T(8,128)(2,1)} %param.9) | copy-start | bytes 835588
  18.3 26.5 %copy-start.1 = (bf16[512,512]{1,0:T(8,128)(2,1)S(1)}, bf16[512,512]{1,0:T(8,128)(2,1)}, u32[]{:S(2)}) copy-start(bf16[512,512]{1,0:T(8,128)(2,1)} %constant.26.clone.order) | copy-start | bytes 1572868

commit v3 on v2

--- a/solution.py
+++ b/solution.py
@@ -117,7 +117,7 @@
         keep = [lane < 128 - a for a in by]
 
         def turned(c, t, m):
-            return pltpu.roll(mask[c, t, pl.ds(first[m], 32), :], turn[m], 1)
+            return pltpu.roll(mask[c, t, pl.ds(first[m], 32), :].astype(BF16), turn[m], 1)
 
         before = [[turned(c, 0, m) for c in range(2)] for m in range(2)]
         for t in range(8):
@@ -125,13 +125,14 @@
             pr, pi = share[0, t], share[1, t]
             for m in range(2):
                 after = [turned(c, t + 1, m) for c in range(2)]
-                wr, wi = [jnp.where(keep[m], before[m][c], after[c]) for c in range(2)]
+                parts = [jnp.where(keep[m], before[m][c], after[c]) for c in range(2)]
+                wr, wi = [part.astype(F32) for part in parts]
                 before[m] = after
                 low, high = m * 32, 64 + m * 32
                 field[at + low : at + low + 32, cols] = (pr * wr - pi * wi).astype(BF16)
                 field[at + high : at + high + 32, cols] = (pr * wi + pi * wr).astype(BF16)
-                windows[p, low : low + 32, cols] = wr.astype(BF16)
-                windows[p, high : high + 32, cols] = wi.astype(BF16)
+                windows[p, low : low + 32, cols] = parts[0]
+                windows[p, high : high + 32, cols] = parts[1]
 
     def transform(g, field):
         mixed = []
@@ -165,15 +166,17 @@
 
 def image_kernel(x, order, table, measured, roots, y, intensity, left, back, parts):
     sign = lane_sign((128, 128))
+    stacked = []
     for q in range(4):
         tiles = []
         for rr in range(4):
             r = 4 * q + rr
             tiles.append(jnp.concatenate(swap_halves(x[r].astype(F32), x[16 + r].astype(F32)), axis=0))
-        lined = jnp.concatenate(tiles, axis=1).astype(BF16)
-        sorted_lanes = jnp.dot(lined, order[...], preferred_element_type=F32)
+        stacked.append(jnp.concatenate(tiles, axis=1).astype(BF16))
+    sorted_lanes = jnp.dot(jnp.concatenate(stacked, axis=0), order[...], preferred_element_type=F32)
+    for q in range(4):
         for f0 in range(4):
-            tile = sorted_lanes[:, f0 * 128 : (f0 + 1) * 128]
+            tile = sorted_lanes[q * 128 : (q + 1) * 128, f0 * 128 : (f0 + 1) * 128]
             left[f0, 0:128, q * 128 : (q + 1) * 128] = (tile * sign).astype(BF16)
             left[f0, 128:256, q * 128 : (q + 1) * 128] = pltpu.roll(tile, 64, 1).astype(BF16)
 
@@ -206,10 +209,10 @@
             cols = slice(q * 128, (q + 1) * 128)
             mixed = sign * both[:128, cols] + pltpu.roll(both[128:, cols], 64, 1)
             parts[q, :, f0 * 128 : (f0 + 1) * 128] = (mixed * roots[...]).astype(BF16)
+    lined = lax.dot_general(parts[...].reshape(512, 512), order[...], NT, preferred_element_type=F32)
     for q in range(4):
-        lined = lax.dot_general(parts[q], order[...], NT, preferred_element_type=F32)
         for rr in range(4):
-            tile = lined[:, rr * 128 : (rr + 1) * 128]
+            tile = lined[q * 128 : (q + 1) * 128, rr * 128 : (rr + 1) * 128]
             low, high = swap_halves(tile[:64], tile[64:])
             y[4 * q + rr] = low.astype(BF16)
             y[16 + 4 * q + rr] = high.astype(BF16)
@@ -217,32 +220,29 @@
 
 def gradient_kernel(y, table, windows, intensity, out, total):
     sign = lane_sign((128, 128))
-    total[...] = jnp.zeros_like(total)
-
-    def group(g, carry):
-        tiles = [y[:, n, pl.ds(pl.multiple_of(g * 16, 16), 16), :].astype(F32) for n in range(2)]
-        lefts = []
+    lefts = []
+    for g in range(4):
+        tiles = [y[:, n, g * 16 : (g + 1) * 16, :].astype(F32) for n in range(2)]
         for half in range(2):
             part = slice(half * 8, (half + 1) * 8)
             for u in swap_rows(tiles[0][:, part], tiles[1][:, part]):
                 u = u.reshape(128, 128)
                 lefts.append(jnp.concatenate([u, sign * pltpu.roll(u, 64, 1)], axis=0).astype(BF16))
-        left = jnp.concatenate(lefts, axis=1)
-        for n in range(4):
-            cols = slice(n * 256, (n + 1) * 256)
+    for n in range(4):
+        cols = slice(n * 256, (n + 1) * 256)
+        real = imag = 0.0
+        for g in range(4):
+            left = jnp.concatenate(lefts[4 * g : 4 * g + 4], axis=1)
             v = lax.dot_general(left, table[:, cols], TN, preferred_element_type=F32)
-            real, imag = total[0:64, cols], total[64:128, cols]
             for m in range(4):
                 vr, vi = v[m * 128 : m * 128 + 64], v[m * 128 + 64 : m * 128 + 128]
                 w = windows[4 * g + m, :, cols].astype(F32)
                 wr, wi = w[:64], w[64:]
-                real = real + wr * vr + wi * vi
-                imag = imag + wr * vi - wi * vr
-            total[0:64, cols] = real
-            total[64:128, cols] = imag
-        return carry
-
-    lax.fori_loop(0, 4, group, 0)
+                real = real + (wr * vr + wi * vi)
+                imag = imag + (wr * vi - wi * vr)
+        total[0:64, cols] = real
+        total[64:128, cols] = imag
+
     for t in range(8):
         cols = slice(t * 128, (t + 1) * 128)
         real = total[0:32, cols] + total[32:64, cols]

time: 83.6 us -> 82 us (0.981)
  Pallas kernels: 16 us -> 14.4 us
where the time goes in v3:
time: 82 us; the launch traced here: 81.5 us
  blocking collectives  46.3 us (56%)
  Pallas kernels  14.4 us (18%)
  starting transfers between devices  13.2 us (16%)
  waiting for transfers between devices  3.77 us (5%)
  local copies, waits for them, and re-layouts  3.09 us (4%)
    all_to_all x3, blocking collectives, exchange(): return lax.all_to_all(blocks, axes, split_axis=0, concat_axis=0, tiled=True)  46.3 us
    all_to_all x1, starting transfers between devices, exchange(): return lax.all_to_all(blocks, axes, split_axis=0, concat_axis=0, tiled=True)  8.7 us
    ppermute x1, starting transfers between devices, shards(): beyond = lax.ppermute(late, 'row', [(i + 1, i) for i in range(NROW - 1)])  4.5 us
    pallas_call x1, Pallas kernels, image_call(): pl.pallas_call(image_kernel, out_shape=(jax.ShapeDtypeStruct((DEST, 64, 1...  4.15 us
    pallas_call x1, Pallas kernels, rows_call(): pl.pallas_call(rows_kernel, out_shape=(jax.ShapeDtypeStruct((16, 2, 64, 1...  3.97 us
    all_to_all x1, waiting for transfers between devices, exchange(): return lax.all_to_all(blocks, axes, split_axis=0, concat_axis=0, tiled=True)  3.77 us
    pallas_call x1, Pallas kernels, gradient_call(): pl.pallas_call(gradient_kernel, out_shape=jax.ShapeDtypeStruct((16, 48, 1...  2.76 us
    unnamed x6, local copies, waits for them, and re-layouts  2.01 us
  transfers between devices with their start and end apart: 2, of which 1 were waited for; matrix products, arithmetic and copies ran while one was open for 1% of the time, Pallas kernels for 2%

profile of v3, /device:TPU:2, one launch (start us, length us, event | category | flops | bytes accessed | tf_op | source)
XLA Modules:
  0.0 81.5 jit_solution(8774142778012828303)
XLA Ops:
  0.6 1.3 %own.1 = f32[16,1,128]{2,1,0:T(1,128)} custom-call(s32[2,2]{1,0:T(2,128)} %shifts.1, f32[2]{0:T(128)} %weights.1), custom_call_target="tpu_custom_call" | custom-call | tf_op jit(solution)/shard_map/own/pallas_call | solution.py:302
  1.9 4.5 %collective-permute-start = (bf16[2,64,1088]{2,1,0:T(8,128)(2,1)}, bf16[2,64,1088]{2,1,0:T(8,128)(2,1)S(1)}, u32[]{:S(2)}, u32[]{:S(2)}) collective-permute-start(bf16[2,64,1088]{2,1,0:T(8,128)(2,1)} %bitcast.11), channel_id=1, source_target_pairs={{1,0},{2,1},{3,2},{4,3},{5,4},{6,5},{7,6},{8,7},{9,8},{10,9},{11,1... | collective-permute-start | bytes 835592 | tf_op jit(solution)/shard_map/ppermute | solution.py:402
  6.4 8.7 %all-to-all-start = ((f32[16,1,128]{2,1,0:T(1,128)}), f32[16,1,128]{2,1,0:T(1,128)S(1)}, u32[]{:S(2)}, u32[]{:S(2)}) async-start(f32[16,1,128]{2,1,0:T(1,128)} %own.1), calls=%async_computation | async-start | bytes 16384 | tf_op jit(solution)/shard_map/all_to_all | solution.py:394
  15.2 1.1 %dynamic-slice_bitcast_fusion.table = bf16[256,1024]{1,0:T(8,128)(2,1)S(1)} fusion(bf16[8,256,1024]{2,1,0:T(8,128)(2,1)} %constant.24.clone, s32[]{:T(128)S(6)} %select_n.4), kind=kLoop, calls=%fused_computation | loop fusion | bytes 1048580 | tf_op jit(solution)/shard_map/jit(dynamic_index_in_dim)/squeeze | solution.py:405
  16.2 0.1 pad_add_fusion.place
  16.3 0.0 copy-start
  16.3 1.0 %copy-done = f32[2,1024,64]{1,2,0:T(8,128)S(1)} copy-done((f32[2,1024,64]{1,2,0:T(8,128)S(1)}, f32[2,1024,64]{1,2,0:T(8,128)}, u32[]{:S(2)}) %copy-start) | copy-done | bytes 524312
  17.4 0.0 copy-start.2
  17.4 1.0 %copy-done.2 = bf16[2,1088,64]{1,2,0:T(8,128)(2,1)S(1)} copy-done((bf16[2,1088,64]{1,2,0:T(8,128)(2,1)S(1)}, bf16[2,1088,64]{1,2,0:T(8,128)(2,1)}, u32[]{:S(2)}) %copy-start.2) | copy-done | bytes 278552
  18.3 0.0 copy-start.1
  18.3 1.5 %stage.1 = (f32[2,9,64,128]{3,2,1,0:T(8,128)S(1)}, f32[2,8,32,128]{3,2,1,0:T(8,128)S(1)}, f32[8,4096]{1,0:T(8,128)S(1)}) custom-call(s32[2]{0:T(128)S(1)} %pad_add_fusion.place, bf16[2,64,1088]{2,1,0:T(8,128)(2,1)S(1)} %bitcast.12, f32[2,64,1024]{2,1,0:T(8,128)S(1)} %bitcast.10, f32[64,4096]{1,0:T(8,128)} %measured.1), custom_call_target="tpu_custom_call" | custom-call | tf_op jit(solution)/shard_map/stage/pallas_call | solution.py:312
  19.8 3.8 %all-to-all-done.gathered = f32[16,1,128]{2,1,0:T(1,128)S(1)} async-done(((f32[16,1,128]{2,1,0:T(1,128)}), f32[16,1,128]{2,1,0:T(1,128)S(1)}, u32[]{:S(2)}, u32[]{:S(2)}) %all-to-all-start) | async-done | bytes 8224 | tf_op jit(solution)/shard_map/all_to_all | solution.py:394
  23.6 0.0 collective-permute-done.beyond
  23.6 4.0 %rows.1 = (bf16[16,2,64,128]{3,2,1,0:T(8,128)(2,1)S(1)}, bf16[16,128,1024]{2,1,0:T(8,128)(2,1)S(1)}, f32[128,128]{1,0:T(8,128)S(1)}, bf16[4,512,1024]{2,1,0:T(8,128)(2,1)S(1)}) custom-call(f32[16,1,128]{2,1,0:T(1,128)S(1)} %all-to-all-done.gathered, bf16[256,1024]{1,0:T(8,128)(2,1)S(1)} %dynamic-slice_bitcast_fusion.table, ...), custom_call_target="tpu_custom_call" | custom-call | tf_op jit(solution)/shard_map/rows/pallas_call | solution.py:329
  27.6 16.8 %all_to_all.20.x = bf16[32,64,128]{2,1,0:T(8,128)(2,1)S(1)} all-to-all(bf16[32,64,128]{2,1,0:T(8,128)(2,1)S(1)} %bitcast.9), channel_id=1, replica_groups=mesh['z'=8,'yl'=2,'row'=16] {'yl','row'}, dimensions={0} | all-to-all | bytes 1048576 | tf_op jit(solution)/shard_map/all_to_all | solution.py:394
  44.4 0.0 copy-done.1
  44.4 4.1 %image.1 = (bf16[32,64,128]{2,1,0:T(8,128)(2,1)S(1)}, f32[16,8,128]{2,1,0:T(8,128)S(1)}) custom-call(bf16[32,64,128]{2,1,0:T(8,128)(2,1)S(1)} %all_to_all.20.x, bf16[512,512]{1,0:T(8,128)(2,1)S(1)} %copy-done.1, bf16[4,512,1024]{2,1,0:T(8,128)(2,1)S(1)} %get-tuple-element.18.table, f32[8,4096]{1,0:T(8,128)S(1)} %get-tuple-element.19.measured, ...), custom_call_target="tpu_custom_call" | custom-call | tf_op jit(solution)/shard_map/image/pallas_call | solution.py:352
  48.5 15.1 %all_to_all.21 = bf16[32,64,128]{2,1,0:T(8,128)(2,1)S(1)} all-to-all(bf16[32,64,128]{2,1,0:T(8,128)(2,1)S(1)} %get-tuple-element.21), channel_id=1, replica_groups=mesh['z'=8,'yl'=2,'row'=16] {'yl','row'}, dimensions={0} | all-to-all | bytes 1048576 | tf_op jit(solution)/shard_map/all_to_all | solution.py:394
  63.7 2.8 %gradient.1 = bf16[16,48,128]{2,1,0:T(8,128)(2,1)S(1)} custom-call(bf16[16,2,64,128]{3,2,1,0:T(8,128)(2,1)S(1)} %bitcast.8, bf16[256,1024]{1,0:T(8,128)(2,1)S(1)} %dynamic-slice_bitcast_fusion.table, bf16[16,128,1024]{2,1,0:T(8,128)(2,1)S(1)} %get-tuple-element.22.windows, f32[16,8,128]{2,1,0:T(8,128)S(1)} %get-tuple-element.23.intensity), custom_call_target="tpu_custom_call" | custom-call | tf_op jit(solution)/shard_map/gradient/pallas_call | solution.py:371
  66.4 14.4 %all_to_all.22.parts = bf16[16,48,128]{2,1,0:T(8,128)(2,1)S(1)} all-to-all(bf16[16,48,128]{2,1,0:T(8,128)(2,1)S(1)} %gradient.1), channel_id=1, replica_groups=mesh['z'=8,'yl'=2,'row'=16] {'z','yl'}, dimensions={0} | all-to-all | bytes 393216 | tf_op jit(solution)/shard_map/all_to_all | solution.py:394
  80.8 0.7 final.1
Async XLA Ops:
  1.9 21.6 %collective-permute-start = (bf16[2,64,1088]{2,1,0:T(8,128)(2,1)}, bf16[2,64,1088]{2,1,0:T(8,128)(2,1)S(1)}, u32[]{:S(2)}, u32[]{:S(2)}) collective-permute-start(bf16[2,64,1088]{2,1,0:T(8,128)(2,1)} %bitcast.11), channel_id=1, source_target_pairs={{1,0},{2,1},{3,2},{4,3},{5,4},{6,5},{7,6},{8,7},{9,8},{10,9},{11,1... | collective-permute-start | bytes 835592 | tf_op jit(solution)/shard_map/ppermute | solution.py:402
  6.4 17.1 %all-to-all-start = ((f32[16,1,128]{2,1,0:T(1,128)}), f32[16,1,128]{2,1,0:T(1,128)S(1)}, u32[]{:S(2)}, u32[]{:S(2)}) async-start(f32[16,1,128]{2,1,0:T(1,128)} %own.1), calls=%async_computation | async-start | bytes 16384 | tf_op jit(solution)/shard_map/all_to_all | solution.py:394
  16.3 1.0 %copy-start = (f32[2,1024,64]{1,2,0:T(8,128)S(1)}, f32[2,1024,64]{1,2,0:T(8,128)}, u32[]{:S(2)}) copy-start(f32[2,1024,64]{1,2,0:T(8,128)} %param.8) | copy-start | bytes 1572868
  17.4 1.0 %copy-start.2 = (bf16[2,1088,64]{1,2,0:T(8,128)(2,1)S(1)}, bf16[2,1088,64]{1,2,0:T(8,128)(2,1)}, u32[]{:S(2)}) copy-start(bf16[2,1088,64]{1,2,0:T(8,128)(2,1)} %param.9) | copy-start | bytes 835588
  18.3 26.0 %copy-start.1 = (bf16[512,512]{1,0:T(8,128)(2,1)S(1)}, bf16[512,512]{1,0:T(8,128)(2,1)}, u32[]{:S(2)}) copy-start(bf16[512,512]{1,0:T(8,128)(2,1)} %constant.26.clone.order) | copy-start | bytes 1572868

commit v4 on v3

--- a/solution.py
+++ b/solution.py
@@ -171,14 +171,14 @@
         tiles = []
         for rr in range(4):
             r = 4 * q + rr
-            tiles.append(jnp.concatenate(swap_halves(x[r].astype(F32), x[16 + r].astype(F32)), axis=0))
-        stacked.append(jnp.concatenate(tiles, axis=1).astype(BF16))
+            tiles.append(jnp.concatenate(swap_halves(x[r], x[16 + r]), axis=0))
+        stacked.append(jnp.concatenate(tiles, axis=1))
     sorted_lanes = jnp.dot(jnp.concatenate(stacked, axis=0), order[...], preferred_element_type=F32)
     for q in range(4):
         for f0 in range(4):
             tile = sorted_lanes[q * 128 : (q + 1) * 128, f0 * 128 : (f0 + 1) * 128]
             left[f0, 0:128, q * 128 : (q + 1) * 128] = (tile * sign).astype(BF16)
-            left[f0, 128:256, q * 128 : (q + 1) * 128] = pltpu.roll(tile, 64, 1).astype(BF16)
+            left[f0, 128:256, q * 128 : (q + 1) * 128] = pltpu.roll(tile.astype(BF16), 64, 1)
 
     upper = lax.broadcasted_iota(jnp.int32, (8, 128), 0) < 4
     for n in range(4):
@@ -212,22 +212,20 @@
     lined = lax.dot_general(parts[...].reshape(512, 512), order[...], NT, preferred_element_type=F32)
     for q in range(4):
         for rr in range(4):
-            tile = lined[q * 128 : (q + 1) * 128, rr * 128 : (rr + 1) * 128]
-            low, high = swap_halves(tile[:64], tile[64:])
-            y[4 * q + rr] = low.astype(BF16)
-            y[16 + 4 * q + rr] = high.astype(BF16)
+            tile = lined[q * 128 : (q + 1) * 128, rr * 128 : (rr + 1) * 128].astype(BF16)
+            y[4 * q + rr], y[16 + 4 * q + rr] = swap_halves(tile[:64], tile[64:])
 
 
 def gradient_kernel(y, table, windows, intensity, out, total):
-    sign = lane_sign((128, 128))
+    sign = lane_sign((128, 128)).astype(BF16)
     lefts = []
     for g in range(4):
         tiles = [y[:, n, g * 16 : (g + 1) * 16, :].astype(F32) for n in range(2)]
         for half in range(2):
             part = slice(half * 8, (half + 1) * 8)
             for u in swap_rows(tiles[0][:, part], tiles[1][:, part]):
-                u = u.reshape(128, 128)
-                lefts.append(jnp.concatenate([u, sign * pltpu.roll(u, 64, 1)], axis=0).astype(BF16))
+                u = u.reshape(128, 128).astype(BF16)
+                lefts.append(jnp.concatenate([u, sign * pltpu.roll(u, 64, 1)], axis=0))
     for n in range(4):
         cols = slice(n * 256, (n + 1) * 256)
         real = imag = 0.0
@@ -250,24 +248,21 @@
         turned = jnp.concatenate([real, imag], axis=0).T
         for n in range(2):
             both = jnp.concatenate([turned[n * 64 : n * 64 + 32], turned[n * 64 + 32 : n * 64 + 64]], axis=1)
-            out[2 * t + n, 0:32] = both.astype(BF16)
-    power = intensity[...]
-    coarse = power.astype(BF16).astype(F32)
-    out[:, 32:48] = jnp.concatenate([coarse, power - coarse], axis=1).astype(BF16)
+            out[2 * t + n, 0:4] = both.reshape(4, 8, 128).astype(BF16)
+    out[:, 4] = intensity[...].astype(BF16)
 
 
 def final_kernel(parts, grad, image):
     for yl in range(2):
         total = jnp.sum(
-            jnp.stack([parts[2 * z + yl, 0:32].astype(F32) for z in range(NZ)]), axis=0
+            jnp.stack([parts[2 * z + yl, 0:4].astype(F32).reshape(32, 128) for z in range(NZ)]), axis=0
         )
         for h in range(2):
             for c in range(2):
                 start = h * 64 + c * 32
                 grad[c, h * 32 : (h + 1) * 32, yl * 32 : (yl + 1) * 32] = total[:, start : start + 32]
     for j in range(16):
-        both = parts[j, 32:48].astype(F32)
-        power = both[:8] + both[8:]
+        power = parts[j, 4].astype(F32)
         for h in range(2):
             image[4 * j : 4 * j + 4, h * 128 : (h + 1) * 128] = power[4 * h : 4 * h + 4]
 
@@ -301,7 +296,7 @@
 def own_call(shifts, weights):
     return pl.pallas_call(
         own_kernel,
-        out_shape=jax.ShapeDtypeStruct((16, 1, 128), F32),
+        out_shape=pltpu.VMEM((16, 1, 128), F32),
         in_specs=[SMEM, SMEM],
         out_specs=vmem(1)[0],
         name="own",
@@ -370,7 +365,7 @@
 def gradient_call(y, table, windows, intensity):
     return pl.pallas_call(
         gradient_kernel,
-        out_shape=jax.ShapeDtypeStruct((16, 48, 128), BF16),
+        out_shape=jax.ShapeDtypeStruct((16, 5, 8, 128), BF16),
         in_specs=vmem(4),
         out_specs=vmem(1)[0],
         scratch_shapes=[pltpu.VMEM((128, K), F32)],
@@ -397,9 +392,8 @@
 def shards(pupil, mask_spectrum, shifts, weights, measured):
     z, yl = lax.axis_index("z"), lax.axis_index("yl")
     mask = mask_spectrum.transpose(0, 2, 1)
-    own, late = lax.optimization_barrier((own_call(shifts, weights), mask))
-    scal = exchange(own, ("z", "yl"))
-    beyond = lax.ppermute(late, "row", [(i + 1, i) for i in range(NROW - 1)])
+    scal = exchange(own_call(shifts, weights), ("z", "yl"))
+    beyond = lax.ppermute(mask, "row", [(i + 1, i) for i in range(NROW - 1)])
     place = jnp.stack([z, yl]).astype(jnp.int32)
     here, share, four = stage_call(place, mask, pupil.transpose(0, 2, 1), measured)
     table = lax.dynamic_index_in_dim(jnp.asarray(row_tables()), z, 0, keepdims=False)

time: 82 us -> 81.4 us (level)
  transfers between devices with their start and end apart: 2 -> 2, of which waited for: 1 -> 1; matrix products, arithmetic and copies ran while one was open for 1% -> 1% of each run, Pallas kernels for 2% -> 3%
where the time goes in v4:
time: 81.4 us; the launch traced here: 81 us
  blocking collectives  45.7 us (56%)
  Pallas kernels  14.5 us (18%)
  starting transfers between devices  13.2 us (16%)
  waiting for transfers between devices  3.77 us (5%)
  local copies, waits for them, and re-layouts  3.09 us (4%)
    all_to_all x3, blocking collectives, exchange(): return lax.all_to_all(blocks, axes, split_axis=0, concat_axis=0, tiled=True)  45.7 us
    all_to_all x1, starting transfers between devices, exchange(): return lax.all_to_all(blocks, axes, split_axis=0, concat_axis=0, tiled=True)  8.68 us
    ppermute x1, starting transfers between devices, shards(): beyond = lax.ppermute(mask, 'row', [(i + 1, i) for i in range(NROW - 1)])  4.52 us
    pallas_call x1, Pallas kernels, image_call(): pl.pallas_call(image_kernel, out_shape=(jax.ShapeDtypeStruct((DEST, 64, 1...  4.16 us
    pallas_call x1, Pallas kernels, rows_call(): pl.pallas_call(rows_kernel, out_shape=(jax.ShapeDtypeStruct((16, 2, 64, 1...  3.98 us
    all_to_all x1, waiting for transfers between devices, exchange(): return lax.all_to_all(blocks, axes, split_axis=0, concat_axis=0, tiled=True)  3.77 us
    pallas_call x1, Pallas kernels, gradient_call(): pl.pallas_call(gradient_kernel, out_shape=jax.ShapeDtypeStruct((16, 5, 8,...  2.8 us
    unnamed x6, local copies, waits for them, and re-layouts  2.01 us
  transfers between devices with their start and end apart: 2, of which 1 were waited for; matrix products, arithmetic and copies ran while one was open for 1% of the time, Pallas kernels for 3%

profile of v4, /device:TPU:2, one launch (start us, length us, event | category | flops | bytes accessed | tf_op | source)
XLA Modules:
  0.0 81.0 jit_solution(14856729649066235390)
XLA Ops:
  0.6 4.5 %collective-permute-start = (bf16[2,64,1088]{2,1,0:T(8,128)(2,1)}, bf16[2,64,1088]{2,1,0:T(8,128)(2,1)S(1)}, u32[]{:S(2)}, u32[]{:S(2)}) collective-permute-start(bf16[2,64,1088]{2,1,0:T(8,128)(2,1)} %bitcast.11), channel_id=1, source_target_pairs={{1,0},{2,1},{3,2},{4,3},{5,4},{6,5},{7,6},{8,7},{9,8},{10,9},{11,1... | collective-permute-start | bytes 835592 | tf_op jit(solution)/shard_map/ppermute | solution.py:396
  5.2 1.3 %own.1 = f32[16,1,128]{2,1,0:T(1,128)} custom-call(s32[2,2]{1,0:T(2,128)} %shifts.1, f32[2]{0:T(128)} %weights.1), custom_call_target="tpu_custom_call" | custom-call | tf_op jit(solution)/shard_map/own/pallas_call | solution.py:297
  6.5 8.7 %all-to-all-start = ((f32[16,1,128]{2,1,0:T(1,128)}), f32[16,1,128]{2,1,0:T(1,128)S(1)}, u32[]{:S(2)}, u32[]{:S(2)}) async-start(f32[16,1,128]{2,1,0:T(1,128)} %own.1), calls=%async_computation | async-start | bytes 16384 | tf_op jit(solution)/shard_map/all_to_all | solution.py:389
  15.2 1.1 %dynamic-slice_bitcast_fusion.table = bf16[256,1024]{1,0:T(8,128)(2,1)S(1)} fusion(bf16[8,256,1024]{2,1,0:T(8,128)(2,1)} %constant.24.clone, s32[]{:T(128)S(6)} %select_n.4), kind=kLoop, calls=%fused_computation | loop fusion | bytes 1048580 | tf_op jit(solution)/shard_map/jit(dynamic_index_in_dim)/squeeze | solution.py:399
  16.2 0.1 pad_add_fusion.place
  16.3 0.0 copy-start
  16.3 1.0 %copy-done = f32[2,1024,64]{1,2,0:T(8,128)S(1)} copy-done((f32[2,1024,64]{1,2,0:T(8,128)S(1)}, f32[2,1024,64]{1,2,0:T(8,128)}, u32[]{:S(2)}) %copy-start) | copy-done | bytes 524312
  17.4 0.0 copy-start.2
  17.4 1.0 %copy-done.2 = bf16[2,1088,64]{1,2,0:T(8,128)(2,1)S(1)} copy-done((bf16[2,1088,64]{1,2,0:T(8,128)(2,1)S(1)}, bf16[2,1088,64]{1,2,0:T(8,128)(2,1)}, u32[]{:S(2)}) %copy-start.2) | copy-done | bytes 278552
  18.3 0.0 copy-start.1
  18.3 1.5 %stage.1 = (f32[2,9,64,128]{3,2,1,0:T(8,128)S(1)}, f32[2,8,32,128]{3,2,1,0:T(8,128)S(1)}, f32[8,4096]{1,0:T(8,128)S(1)}) custom-call(s32[2]{0:T(128)S(1)} %pad_add_fusion.place, bf16[2,64,1088]{2,1,0:T(8,128)(2,1)S(1)} %bitcast.12, f32[2,64,1024]{2,1,0:T(8,128)S(1)} %bitcast.10, f32[64,4096]{1,0:T(8,128)} %measured.1), custom_call_target="tpu_custom_call" | custom-call | tf_op jit(solution)/shard_map/stage/pallas_call | solution.py:307
  19.8 3.8 %all-to-all-done.gathered = f32[16,1,128]{2,1,0:T(1,128)S(1)} async-done(((f32[16,1,128]{2,1,0:T(1,128)}), f32[16,1,128]{2,1,0:T(1,128)S(1)}, u32[]{:S(2)}, u32[]{:S(2)}) %all-to-all-start) | async-done | bytes 8224 | tf_op jit(solution)/shard_map/all_to_all | solution.py:389
  23.6 0.0 collective-permute-done.beyond
  23.6 4.0 %rows.1 = (bf16[16,2,64,128]{3,2,1,0:T(8,128)(2,1)S(1)}, bf16[16,128,1024]{2,1,0:T(8,128)(2,1)S(1)}, f32[128,128]{1,0:T(8,128)S(1)}, bf16[4,512,1024]{2,1,0:T(8,128)(2,1)S(1)}) custom-call(f32[16,1,128]{2,1,0:T(1,128)S(1)} %all-to-all-done.gathered, bf16[256,1024]{1,0:T(8,128)(2,1)S(1)} %dynamic-slice_bitcast_fusion.table, ...), custom_call_target="tpu_custom_call" | custom-call | tf_op jit(solution)/shard_map/rows/pallas_call | solution.py:324
  27.6 16.8 %all_to_all.20.x = bf16[32,64,128]{2,1,0:T(8,128)(2,1)S(1)} all-to-all(bf16[32,64,128]{2,1,0:T(8,128)(2,1)S(1)} %bitcast.9), channel_id=1, replica_groups=mesh['z'=8,'yl'=2,'row'=16] {'yl','row'}, dimensions={0} | all-to-all | bytes 1048576 | tf_op jit(solution)/shard_map/all_to_all | solution.py:389
  44.4 0.0 copy-done.1
  44.4 4.2 %image.1 = (bf16[32,64,128]{2,1,0:T(8,128)(2,1)S(1)}, f32[16,8,128]{2,1,0:T(8,128)S(1)}) custom-call(bf16[32,64,128]{2,1,0:T(8,128)(2,1)S(1)} %all_to_all.20.x, bf16[512,512]{1,0:T(8,128)(2,1)S(1)} %copy-done.1, bf16[4,512,1024]{2,1,0:T(8,128)(2,1)S(1)} %get-tuple-element.14.table, f32[8,4096]{1,0:T(8,128)S(1)} %get-tuple-element.15.measured, ...), custom_call_target="tpu_custom_call" | custom-call | tf_op jit(solution)/shard_map/image/pallas_call | solution.py:347
  48.5 15.1 %all_to_all.21 = bf16[32,64,128]{2,1,0:T(8,128)(2,1)S(1)} all-to-all(bf16[32,64,128]{2,1,0:T(8,128)(2,1)S(1)} %get-tuple-element.17), channel_id=1, replica_groups=mesh['z'=8,'yl'=2,'row'=16] {'yl','row'}, dimensions={0} | all-to-all | bytes 1048576 | tf_op jit(solution)/shard_map/all_to_all | solution.py:389
  63.7 2.8 %gradient.1 = bf16[16,5,8,128]{3,2,1,0:T(8,128)(2,1)S(1)} custom-call(bf16[16,2,64,128]{3,2,1,0:T(8,128)(2,1)S(1)} %bitcast.8, bf16[256,1024]{1,0:T(8,128)(2,1)S(1)} %dynamic-slice_bitcast_fusion.table, bf16[16,128,1024]{2,1,0:T(8,128)(2,1)S(1)} %get-tuple-element.18.windows, f32[16,8,128]{2,1,0:T(8,128)S(1)} %get-tuple-element.19.intensity), custom_call_target="tpu_custom_call" | custom-call | tf_op jit(solution)/shard_map/gradient/pallas_call | solution.py:366
  66.5 13.8 %all_to_all.22.parts = bf16[16,5,8,128]{3,2,1,0:T(8,128)(2,1)S(1)} all-to-all(bf16[16,5,8,128]{3,2,1,0:T(8,128)(2,1)S(1)} %gradient.1), channel_id=1, replica_groups=mesh['z'=8,'yl'=2,'row'=16] {'z','yl'}, dimensions={0} | all-to-all | bytes 327680 | tf_op jit(solution)/shard_map/all_to_all | solution.py:389
  80.2 0.7 final.1
Async XLA Ops:
  0.6 23.0 %collective-permute-start = (bf16[2,64,1088]{2,1,0:T(8,128)(2,1)}, bf16[2,64,1088]{2,1,0:T(8,128)(2,1)S(1)}, u32[]{:S(2)}, u32[]{:S(2)}) collective-permute-start(bf16[2,64,1088]{2,1,0:T(8,128)(2,1)} %bitcast.11), channel_id=1, source_target_pairs={{1,0},{2,1},{3,2},{4,3},{5,4},{6,5},{7,6},{8,7},{9,8},{10,9},{11,1... | collective-permute-start | bytes 835592 | tf_op jit(solution)/shard_map/ppermute | solution.py:396
  6.5 17.1 %all-to-all-start = ((f32[16,1,128]{2,1,0:T(1,128)}), f32[16,1,128]{2,1,0:T(1,128)S(1)}, u32[]{:S(2)}, u32[]{:S(2)}) async-start(f32[16,1,128]{2,1,0:T(1,128)} %own.1), calls=%async_computation | async-start | bytes 16384 | tf_op jit(solution)/shard_map/all_to_all | solution.py:389
  16.3 1.0 %copy-start = (f32[2,1024,64]{1,2,0:T(8,128)S(1)}, f32[2,1024,64]{1,2,0:T(8,128)}, u32[]{:S(2)}) copy-start(f32[2,1024,64]{1,2,0:T(8,128)} %param.8) | copy-start | bytes 1572868
  17.4 1.0 %copy-start.2 = (bf16[2,1088,64]{1,2,0:T(8,128)(2,1)S(1)}, bf16[2,1088,64]{1,2,0:T(8,128)(2,1)}, u32[]{:S(2)}) copy-start(bf16[2,1088,64]{1,2,0:T(8,128)(2,1)} %param.9) | copy-start | bytes 835588
  18.3 26.0 %copy-start.1 = (bf16[512,512]{1,0:T(8,128)(2,1)S(1)}, bf16[512,512]{1,0:T(8,128)(2,1)}, u32[]{:S(2)}) copy-start(bf16[512,512]{1,0:T(8,128)(2,1)} %constant.26.clone.order) | copy-start | bytes 1572868

commit v5 on v4

--- a/solution.py
+++ b/solution.py
@@ -248,21 +248,23 @@
         turned = jnp.concatenate([real, imag], axis=0).T
         for n in range(2):
             both = jnp.concatenate([turned[n * 64 : n * 64 + 32], turned[n * 64 + 32 : n * 64 + 64]], axis=1)
-            out[2 * t + n, 0:4] = both.reshape(4, 8, 128).astype(BF16)
-    out[:, 4] = intensity[...].astype(BF16)
+            out[8 * n + t, 0:4] = both.reshape(4, 8, 128).astype(BF16)
+    for yl in range(2):
+        for z in range(8):
+            out[8 * yl + z, 4] = intensity[2 * z + yl].astype(BF16)
 
 
 def final_kernel(parts, grad, image):
     for yl in range(2):
         total = jnp.sum(
-            jnp.stack([parts[2 * z + yl, 0:4].astype(F32).reshape(32, 128) for z in range(NZ)]), axis=0
+            jnp.stack([parts[8 * yl + z, 0:4].astype(F32).reshape(32, 128) for z in range(NZ)]), axis=0
         )
         for h in range(2):
             for c in range(2):
                 start = h * 64 + c * 32
                 grad[c, h * 32 : (h + 1) * 32, yl * 32 : (yl + 1) * 32] = total[:, start : start + 32]
     for j in range(16):
-        power = parts[j, 4].astype(F32)
+        power = parts[j % 2 * 8 + j // 2, 4].astype(F32)
         for h in range(2):
             image[4 * j : 4 * j + 4, h * 128 : (h + 1) * 128] = power[4 * h : 4 * h + 4]
 
@@ -400,7 +402,7 @@
     blocks, windows, roots, near = rows_call(scal, table, here, beyond, share)
     blocks, intensity = image_call(exchange(blocks.reshape(DEST, 64, 128), ("yl", "row")), near, four, roots)
     blocks = exchange(blocks, ("yl", "row"))
-    parts = exchange(gradient_call(blocks, table, windows, intensity), ("z", "yl"))
+    parts = exchange(gradient_call(blocks, table, windows, intensity), ("yl", "z"))
     return final_call(parts)
 
 

time: 81.4 us -> 80.4 us (0.988)
  blocking collectives: 45.7 us -> 44.1 us
    all_to_all x3, blocking collectives: 45.7 us -> 44.1 us  [exchange(): return lax.all_to_all(blocks, axes, split_axis=0, concat_axis=0, tiled=True)]
where the time goes in v5:
time: 80.4 us; the launch traced here: 79.4 us
  blocking collectives  44.1 us (55%)
  Pallas kernels  14.5 us (18%)
  starting transfers between devices  13.2 us (16%)
  waiting for transfers between devices  3.77 us (5%)
  local copies, waits for them, and re-layouts  3.09 us (4%)
    all_to_all x3, blocking collectives, exchange(): return lax.all_to_all(blocks, axes, split_axis=0, concat_axis=0, tiled=True)  44.1 us
    all_to_all x1, starting transfers between devices, exchange(): return lax.all_to_all(blocks, axes, split_axis=0, concat_axis=0, tiled=True)  8.68 us
    ppermute x1, starting transfers between devices, shards(): beyond = lax.ppermute(mask, 'row', [(i + 1, i) for i in range(NROW - 1)])  4.52 us
    pallas_call x1, Pallas kernels, image_call(): pl.pallas_call(image_kernel, out_shape=(jax.ShapeDtypeStruct((DEST, 64, 1...  4.16 us
    pallas_call x1, Pallas kernels, rows_call(): pl.pallas_call(rows_kernel, out_shape=(jax.ShapeDtypeStruct((16, 2, 64, 1...  3.99 us
    all_to_all x1, waiting for transfers between devices, exchange(): return lax.all_to_all(blocks, axes, split_axis=0, concat_axis=0, tiled=True)  3.77 us
    pallas_call x1, Pallas kernels, gradient_call(): pl.pallas_call(gradient_kernel, out_shape=jax.ShapeDtypeStruct((16, 5, 8,...  2.81 us
    unnamed x6, local copies, waits for them, and re-layouts  2.01 us
  transfers between devices with their start and end apart: 2, of which 1 were waited for; matrix products, arithmetic and copies ran while one was open for 1% of the time, Pallas kernels for 3%

profile of v5, /device:TPU:2, one launch (start us, length us, event | category | flops | bytes accessed | tf_op | source)
XLA Modules:
  0.0 79.4 jit_solution(7994018410073128445)
XLA Ops:
  0.6 4.5 %collective-permute-start = (bf16[2,64,1088]{2,1,0:T(8,128)(2,1)}, bf16[2,64,1088]{2,1,0:T(8,128)(2,1)S(1)}, u32[]{:S(2)}, u32[]{:S(2)}) collective-permute-start(bf16[2,64,1088]{2,1,0:T(8,128)(2,1)} %bitcast.11), channel_id=1, source_target_pairs={{1,0},{2,1},{3,2},{4,3},{5,4},{6,5},{7,6},{8,7},{9,8},{10,9},{11,1... | collective-permute-start | bytes 835592 | tf_op jit(solution)/shard_map/ppermute | solution.py:398
  5.2 1.3 %own.1 = f32[16,1,128]{2,1,0:T(1,128)} custom-call(s32[2,2]{1,0:T(2,128)} %shifts.1, f32[2]{0:T(128)} %weights.1), custom_call_target="tpu_custom_call" | custom-call | tf_op jit(solution)/shard_map/own/pallas_call | solution.py:299
  6.5 8.7 %all-to-all-start = ((f32[16,1,128]{2,1,0:T(1,128)}), f32[16,1,128]{2,1,0:T(1,128)S(1)}, u32[]{:S(2)}, u32[]{:S(2)}) async-start(f32[16,1,128]{2,1,0:T(1,128)} %own.1), calls=%async_computation | async-start | bytes 16384 | tf_op jit(solution)/shard_map/all_to_all | solution.py:391
  15.2 1.1 %dynamic-slice_bitcast_fusion.table = bf16[256,1024]{1,0:T(8,128)(2,1)S(1)} fusion(bf16[8,256,1024]{2,1,0:T(8,128)(2,1)} %constant.24.clone, s32[]{:T(128)S(6)} %select_n.4), kind=kLoop, calls=%fused_computation | loop fusion | bytes 1048580 | tf_op jit(solution)/shard_map/jit(dynamic_index_in_dim)/squeeze | solution.py:401
  16.2 0.1 pad_add_fusion.place
  16.3 0.0 copy-start
  16.3 1.0 %copy-done = f32[2,1024,64]{1,2,0:T(8,128)S(1)} copy-done((f32[2,1024,64]{1,2,0:T(8,128)S(1)}, f32[2,1024,64]{1,2,0:T(8,128)}, u32[]{:S(2)}) %copy-start) | copy-done | bytes 524312
  17.4 0.0 copy-start.2
  17.4 1.0 %copy-done.2 = bf16[2,1088,64]{1,2,0:T(8,128)(2,1)S(1)} copy-done((bf16[2,1088,64]{1,2,0:T(8,128)(2,1)S(1)}, bf16[2,1088,64]{1,2,0:T(8,128)(2,1)}, u32[]{:S(2)}) %copy-start.2) | copy-done | bytes 278552
  18.3 0.0 copy-start.1
  18.3 1.5 %stage.1 = (f32[2,9,64,128]{3,2,1,0:T(8,128)S(1)}, f32[2,8,32,128]{3,2,1,0:T(8,128)S(1)}, f32[8,4096]{1,0:T(8,128)S(1)}) custom-call(s32[2]{0:T(128)S(1)} %pad_add_fusion.place, bf16[2,64,1088]{2,1,0:T(8,128)(2,1)S(1)} %bitcast.12, f32[2,64,1024]{2,1,0:T(8,128)S(1)} %bitcast.10, f32[64,4096]{1,0:T(8,128)} %measured.1), custom_call_target="tpu_custom_call" | custom-call | tf_op jit(solution)/shard_map/stage/pallas_call | solution.py:309
  19.8 3.8 %all-to-all-done.gathered = f32[16,1,128]{2,1,0:T(1,128)S(1)} async-done(((f32[16,1,128]{2,1,0:T(1,128)}), f32[16,1,128]{2,1,0:T(1,128)S(1)}, u32[]{:S(2)}, u32[]{:S(2)}) %all-to-all-start) | async-done | bytes 8224 | tf_op jit(solution)/shard_map/all_to_all | solution.py:391
  23.6 0.0 collective-permute-done.beyond
  23.6 4.0 %rows.1 = (bf16[16,2,64,128]{3,2,1,0:T(8,128)(2,1)S(1)}, bf16[16,128,1024]{2,1,0:T(8,128)(2,1)S(1)}, f32[128,128]{1,0:T(8,128)S(1)}, bf16[4,512,1024]{2,1,0:T(8,128)(2,1)S(1)}) custom-call(f32[16,1,128]{2,1,0:T(1,128)S(1)} %all-to-all-done.gathered, bf16[256,1024]{1,0:T(8,128)(2,1)S(1)} %dynamic-slice_bitcast_fusion.table, ...), custom_call_target="tpu_custom_call" | custom-call | tf_op jit(solution)/shard_map/rows/pallas_call | solution.py:326
  27.6 16.8 %all_to_all.20.x = bf16[32,64,128]{2,1,0:T(8,128)(2,1)S(1)} all-to-all(bf16[32,64,128]{2,1,0:T(8,128)(2,1)S(1)} %bitcast.9), channel_id=1, replica_groups=mesh['z'=8,'yl'=2,'row'=16] {'yl','row'}, dimensions={0} | all-to-all | bytes 1048576 | tf_op jit(solution)/shard_map/all_to_all | solution.py:391
  44.4 0.0 copy-done.1
  44.4 4.2 %image.1 = (bf16[32,64,128]{2,1,0:T(8,128)(2,1)S(1)}, f32[16,8,128]{2,1,0:T(8,128)S(1)}) custom-call(bf16[32,64,128]{2,1,0:T(8,128)(2,1)S(1)} %all_to_all.20.x, bf16[512,512]{1,0:T(8,128)(2,1)S(1)} %copy-done.1, bf16[4,512,1024]{2,1,0:T(8,128)(2,1)S(1)} %get-tuple-element.14.table, f32[8,4096]{1,0:T(8,128)S(1)} %get-tuple-element.15.measured, ...), custom_call_target="tpu_custom_call" | custom-call | tf_op jit(solution)/shard_map/image/pallas_call | solution.py:349
  48.5 15.1 %all_to_all.21 = bf16[32,64,128]{2,1,0:T(8,128)(2,1)S(1)} all-to-all(bf16[32,64,128]{2,1,0:T(8,128)(2,1)S(1)} %get-tuple-element.17), channel_id=1, replica_groups=mesh['z'=8,'yl'=2,'row'=16] {'yl','row'}, dimensions={0} | all-to-all | bytes 1048576 | tf_op jit(solution)/shard_map/all_to_all | solution.py:391
  63.7 2.8 %gradient.1 = bf16[16,5,8,128]{3,2,1,0:T(8,128)(2,1)S(1)} custom-call(bf16[16,2,64,128]{3,2,1,0:T(8,128)(2,1)S(1)} %bitcast.8, bf16[256,1024]{1,0:T(8,128)(2,1)S(1)} %dynamic-slice_bitcast_fusion.table, bf16[16,128,1024]{2,1,0:T(8,128)(2,1)S(1)} %get-tuple-element.18.windows, f32[16,8,128]{2,1,0:T(8,128)S(1)} %get-tuple-element.19.intensity), custom_call_target="tpu_custom_call" | custom-call | tf_op jit(solution)/shard_map/gradient/pallas_call | solution.py:368
  66.5 12.2 %all_to_all.22.parts = bf16[16,5,8,128]{3,2,1,0:T(8,128)(2,1)S(1)} all-to-all(bf16[16,5,8,128]{3,2,1,0:T(8,128)(2,1)S(1)} %gradient.1), channel_id=1, replica_groups=mesh['z'=8,'yl'=2,'row'=16] {'yl','z'}, dimensions={0} | all-to-all | bytes 327680 | tf_op jit(solution)/shard_map/all_to_all | solution.py:391
  78.6 0.7 final.1
Async XLA Ops:
  0.6 23.0 %collective-permute-start = (bf16[2,64,1088]{2,1,0:T(8,128)(2,1)}, bf16[2,64,1088]{2,1,0:T(8,128)(2,1)S(1)}, u32[]{:S(2)}, u32[]{:S(2)}) collective-permute-start(bf16[2,64,1088]{2,1,0:T(8,128)(2,1)} %bitcast.11), channel_id=1, source_target_pairs={{1,0},{2,1},{3,2},{4,3},{5,4},{6,5},{7,6},{8,7},{9,8},{10,9},{11,1... | collective-permute-start | bytes 835592 | tf_op jit(solution)/shard_map/ppermute | solution.py:398
  6.5 17.1 %all-to-all-start = ((f32[16,1,128]{2,1,0:T(1,128)}), f32[16,1,128]{2,1,0:T(1,128)S(1)}, u32[]{:S(2)}, u32[]{:S(2)}) async-start(f32[16,1,128]{2,1,0:T(1,128)} %own.1), calls=%async_computation | async-start | bytes 16384 | tf_op jit(solution)/shard_map/all_to_all | solution.py:391
  16.3 1.0 %copy-start = (f32[2,1024,64]{1,2,0:T(8,128)S(1)}, f32[2,1024,64]{1,2,0:T(8,128)}, u32[]{:S(2)}) copy-start(f32[2,1024,64]{1,2,0:T(8,128)} %param.8) | copy-start | bytes 1572868
  17.4 1.0 %copy-start.2 = (bf16[2,1088,64]{1,2,0:T(8,128)(2,1)S(1)}, bf16[2,1088,64]{1,2,0:T(8,128)(2,1)}, u32[]{:S(2)}) copy-start(bf16[2,1088,64]{1,2,0:T(8,128)(2,1)} %param.9) | copy-start | bytes 835588
  18.3 26.1 %copy-start.1 = (bf16[512,512]{1,0:T(8,128)(2,1)S(1)}, bf16[512,512]{1,0:T(8,128)(2,1)}, u32[]{:S(2)}) copy-start(bf16[512,512]{1,0:T(8,128)(2,1)} %constant.26.clone.order) | copy-start | bytes 1572868

commit v6 on v5

--- a/solution.py
+++ b/solution.py
@@ -35,7 +35,7 @@
 
 @functools.cache
 def row_tables():
-    z, yl, row, i = np.meshgrid(np.arange(NZ), np.arange(NYL), np.arange(NROW), np.arange(4), indexing="ij")
+    z, row, yl, i = np.meshgrid(np.arange(NZ), np.arange(NROW), np.arange(NYL), np.arange(4), indexing="ij")
     x = (64 * row + 8 * z + 4 * yl + i).reshape(NZ, 128, 1)
     cosine, sine = phase(x, np.arange(K) - K // 2)
     return np.concatenate([cosine, sine], axis=1).astype(ml_dtypes.bfloat16)
@@ -171,7 +171,7 @@
         tiles = []
         for rr in range(4):
             r = 4 * q + rr
-            tiles.append(jnp.concatenate(swap_halves(x[r], x[16 + r]), axis=0))
+            tiles.append(jnp.concatenate(swap_halves(x[2 * r], x[2 * r + 1]), axis=0))
         stacked.append(jnp.concatenate(tiles, axis=1))
     sorted_lanes = jnp.dot(jnp.concatenate(stacked, axis=0), order[...], preferred_element_type=F32)
     for q in range(4):
@@ -213,7 +213,7 @@
     for q in range(4):
         for rr in range(4):
             tile = lined[q * 128 : (q + 1) * 128, rr * 128 : (rr + 1) * 128].astype(BF16)
-            y[4 * q + rr], y[16 + 4 * q + rr] = swap_halves(tile[:64], tile[64:])
+            y[8 * q + 2 * rr], y[8 * q + 2 * rr + 1] = swap_halves(tile[:64], tile[64:])
 
 
 def gradient_kernel(y, table, windows, intensity, out, total):
@@ -400,8 +400,8 @@
     here, share, four = stage_call(place, mask, pupil.transpose(0, 2, 1), measured)
     table = lax.dynamic_index_in_dim(jnp.asarray(row_tables()), z, 0, keepdims=False)
     blocks, windows, roots, near = rows_call(scal, table, here, beyond, share)
-    blocks, intensity = image_call(exchange(blocks.reshape(DEST, 64, 128), ("yl", "row")), near, four, roots)
-    blocks = exchange(blocks, ("yl", "row"))
+    blocks, intensity = image_call(exchange(blocks.reshape(DEST, 64, 128), ("row", "yl")), near, four, roots)
+    blocks = exchange(blocks, ("row", "yl"))
     parts = exchange(gradient_call(blocks, table, windows, intensity), ("yl", "z"))
     return final_call(parts)
 

time: 80.4 us -> 79.9 us (level)
  transfers between devices with their start and end apart: 2 -> 2, of which waited for: 1 -> 1; matrix products, arithmetic and copies ran while one was open for 1% -> 1% of each run, Pallas kernels for 3% -> 4%
where the time goes in v6:
time: 79.9 us; the launch traced here: 78.6 us
  blocking collectives  43.3 us (54%)
  Pallas kernels  14.5 us (18%)
  starting transfers between devices  13.2 us (17%)
  waiting for transfers between devices  3.77 us (5%)
  local copies, waits for them, and re-layouts  3.09 us (4%)
    all_to_all x3, blocking collectives, exchange(): return lax.all_to_all(blocks, axes, split_axis=0, concat_axis=0, tiled=True)  43.3 us
    all_to_all x1, starting transfers between devices, exchange(): return lax.all_to_all(blocks, axes, split_axis=0, concat_axis=0, tiled=True)  8.68 us
    ppermute x1, starting transfers between devices, shards(): beyond = lax.ppermute(mask, 'row', [(i + 1, i) for i in range(NROW - 1)])  4.52 us
    pallas_call x1, Pallas kernels, image_call(): pl.pallas_call(image_kernel, out_shape=(jax.ShapeDtypeStruct((DEST, 64, 1...  4.16 us
    pallas_call x1, Pallas kernels, rows_call(): pl.pallas_call(rows_kernel, out_shape=(jax.ShapeDtypeStruct((16, 2, 64, 1...  3.99 us
    all_to_all x1, waiting for transfers between devices, exchange(): return lax.all_to_all(blocks, axes, split_axis=0, concat_axis=0, tiled=True)  3.77 us
    pallas_call x1, Pallas kernels, gradient_call(): pl.pallas_call(gradient_kernel, out_shape=jax.ShapeDtypeStruct((16, 5, 8,...  2.81 us
    unnamed x6, local copies, waits for them, and re-layouts  2.01 us
  transfers between devices with their start and end apart: 2, of which 1 were waited for; matrix products, arithmetic and copies ran while one was open for 1% of the time, Pallas kernels for 4%

profile of v6, /device:TPU:2, one launch (start us, length us, event | category | flops | bytes accessed | tf_op | source)
XLA Modules:
  0.0 78.6 jit_solution(7995077250086602637)
XLA Ops:
  0.6 4.5 %collective-permute-start = (bf16[2,64,1088]{2,1,0:T(8,128)(2,1)}, bf16[2,64,1088]{2,1,0:T(8,128)(2,1)S(1)}, u32[]{:S(2)}, u32[]{:S(2)}) collective-permute-start(bf16[2,64,1088]{2,1,0:T(8,128)(2,1)} %bitcast.11), channel_id=1, source_target_pairs={{1,0},{2,1},{3,2},{4,3},{5,4},{6,5},{7,6},{8,7},{9,8},{10,9},{11,1... | collective-permute-start | bytes 835592 | tf_op jit(solution)/shard_map/ppermute | solution.py:398
  5.2 1.3 %own.1 = f32[16,1,128]{2,1,0:T(1,128)} custom-call(s32[2,2]{1,0:T(2,128)} %shifts.1, f32[2]{0:T(128)} %weights.1), custom_call_target="tpu_custom_call" | custom-call | tf_op jit(solution)/shard_map/own/pallas_call | solution.py:299
  6.5 8.7 %all-to-all-start = ((f32[16,1,128]{2,1,0:T(1,128)}), f32[16,1,128]{2,1,0:T(1,128)S(1)}, u32[]{:S(2)}, u32[]{:S(2)}) async-start(f32[16,1,128]{2,1,0:T(1,128)} %own.1), calls=%async_computation | async-start | bytes 16384 | tf_op jit(solution)/shard_map/all_to_all | solution.py:391
  15.2 1.1 %dynamic-slice_bitcast_fusion.table = bf16[256,1024]{1,0:T(8,128)(2,1)S(1)} fusion(bf16[8,256,1024]{2,1,0:T(8,128)(2,1)} %constant.24.clone, s32[]{:T(128)S(6)} %select_n.4), kind=kLoop, calls=%fused_computation | loop fusion | bytes 1048580 | tf_op jit(solution)/shard_map/jit(dynamic_index_in_dim)/squeeze | solution.py:401
  16.2 0.1 pad_add_fusion.place
  16.3 0.0 copy-start
  16.3 1.0 %copy-done = f32[2,1024,64]{1,2,0:T(8,128)S(1)} copy-done((f32[2,1024,64]{1,2,0:T(8,128)S(1)}, f32[2,1024,64]{1,2,0:T(8,128)}, u32[]{:S(2)}) %copy-start) | copy-done | bytes 524312
  17.4 0.0 copy-start.2
  17.4 1.0 %copy-done.2 = bf16[2,1088,64]{1,2,0:T(8,128)(2,1)S(1)} copy-done((bf16[2,1088,64]{1,2,0:T(8,128)(2,1)S(1)}, bf16[2,1088,64]{1,2,0:T(8,128)(2,1)}, u32[]{:S(2)}) %copy-start.2) | copy-done | bytes 278552
  18.3 0.0 copy-start.1
  18.3 1.5 %stage.1 = (f32[2,9,64,128]{3,2,1,0:T(8,128)S(1)}, f32[2,8,32,128]{3,2,1,0:T(8,128)S(1)}, f32[8,4096]{1,0:T(8,128)S(1)}) custom-call(s32[2]{0:T(128)S(1)} %pad_add_fusion.place, bf16[2,64,1088]{2,1,0:T(8,128)(2,1)S(1)} %bitcast.12, f32[2,64,1024]{2,1,0:T(8,128)S(1)} %bitcast.10, f32[64,4096]{1,0:T(8,128)} %measured.1), custom_call_target="tpu_custom_call" | custom-call | tf_op jit(solution)/shard_map/stage/pallas_call | solution.py:309
  19.8 3.8 %all-to-all-done.gathered = f32[16,1,128]{2,1,0:T(1,128)S(1)} async-done(((f32[16,1,128]{2,1,0:T(1,128)}), f32[16,1,128]{2,1,0:T(1,128)S(1)}, u32[]{:S(2)}, u32[]{:S(2)}) %all-to-all-start) | async-done | bytes 8224 | tf_op jit(solution)/shard_map/all_to_all | solution.py:391
  23.6 0.0 collective-permute-done.beyond
  23.6 4.0 %rows.1 = (bf16[16,2,64,128]{3,2,1,0:T(8,128)(2,1)S(1)}, bf16[16,128,1024]{2,1,0:T(8,128)(2,1)S(1)}, f32[128,128]{1,0:T(8,128)S(1)}, bf16[4,512,1024]{2,1,0:T(8,128)(2,1)S(1)}) custom-call(f32[16,1,128]{2,1,0:T(1,128)S(1)} %all-to-all-done.gathered, bf16[256,1024]{1,0:T(8,128)(2,1)S(1)} %dynamic-slice_bitcast_fusion.table, ...), custom_call_target="tpu_custom_call" | custom-call | tf_op jit(solution)/shard_map/rows/pallas_call | solution.py:326
  27.6 15.9 %all_to_all.20.x = bf16[32,64,128]{2,1,0:T(8,128)(2,1)S(1)} all-to-all(bf16[32,64,128]{2,1,0:T(8,128)(2,1)S(1)} %bitcast.9), channel_id=1, replica_groups=mesh['z'=8,'yl'=2,'row'=16] {'row','yl'}, dimensions={0} | all-to-all | bytes 1048576 | tf_op jit(solution)/shard_map/all_to_all | solution.py:391
  43.5 0.0 copy-done.1
  43.5 4.2 %image.1 = (bf16[32,64,128]{2,1,0:T(8,128)(2,1)S(1)}, f32[16,8,128]{2,1,0:T(8,128)S(1)}) custom-call(bf16[32,64,128]{2,1,0:T(8,128)(2,1)S(1)} %all_to_all.20.x, bf16[512,512]{1,0:T(8,128)(2,1)S(1)} %copy-done.1, bf16[4,512,1024]{2,1,0:T(8,128)(2,1)S(1)} %get-tuple-element.14.table, f32[8,4096]{1,0:T(8,128)S(1)} %get-tuple-element.15.measured, ...), custom_call_target="tpu_custom_call" | custom-call | tf_op jit(solution)/shard_map/image/pallas_call | solution.py:349
  47.7 15.1 %all_to_all.21 = bf16[32,64,128]{2,1,0:T(8,128)(2,1)S(1)} all-to-all(bf16[32,64,128]{2,1,0:T(8,128)(2,1)S(1)} %get-tuple-element.17), channel_id=1, replica_groups=mesh['z'=8,'yl'=2,'row'=16] {'row','yl'}, dimensions={0} | all-to-all | bytes 1048576 | tf_op jit(solution)/shard_map/all_to_all | solution.py:391
  62.7 2.8 %gradient.1 = bf16[16,5,8,128]{3,2,1,0:T(8,128)(2,1)S(1)} custom-call(bf16[16,2,64,128]{3,2,1,0:T(8,128)(2,1)S(1)} %bitcast.8, bf16[256,1024]{1,0:T(8,128)(2,1)S(1)} %dynamic-slice_bitcast_fusion.table, bf16[16,128,1024]{2,1,0:T(8,128)(2,1)S(1)} %get-tuple-element.18.windows, f32[16,8,128]{2,1,0:T(8,128)S(1)} %get-tuple-element.19.intensity), custom_call_target="tpu_custom_call" | custom-call | tf_op jit(solution)/shard_map/gradient/pallas_call | solution.py:368
  65.5 12.3 %all_to_all.22.parts = bf16[16,5,8,128]{3,2,1,0:T(8,128)(2,1)S(1)} all-to-all(bf16[16,5,8,128]{3,2,1,0:T(8,128)(2,1)S(1)} %gradient.1), channel_id=1, replica_groups=mesh['z'=8,'yl'=2,'row'=16] {'yl','z'}, dimensions={0} | all-to-all | bytes 327680 | tf_op jit(solution)/shard_map/all_to_all | solution.py:391
  77.9 0.7 final.1
Async XLA Ops:
  0.6 23.0 %collective-permute-start = (bf16[2,64,1088]{2,1,0:T(8,128)(2,1)}, bf16[2,64,1088]{2,1,0:T(8,128)(2,1)S(1)}, u32[]{:S(2)}, u32[]{:S(2)}) collective-permute-start(bf16[2,64,1088]{2,1,0:T(8,128)(2,1)} %bitcast.11), channel_id=1, source_target_pairs={{1,0},{2,1},{3,2},{4,3},{5,4},{6,5},{7,6},{8,7},{9,8},{10,9},{11,1... | collective-permute-start | bytes 835592 | tf_op jit(solution)/shard_map/ppermute | solution.py:398
  6.5 17.1 %all-to-all-start = ((f32[16,1,128]{2,1,0:T(1,128)}), f32[16,1,128]{2,1,0:T(1,128)S(1)}, u32[]{:S(2)}, u32[]{:S(2)}) async-start(f32[16,1,128]{2,1,0:T(1,128)} %own.1), calls=%async_computation | async-start | bytes 16384 | tf_op jit(solution)/shard_map/all_to_all | solution.py:391
  16.3 1.0 %copy-start = (f32[2,1024,64]{1,2,0:T(8,128)S(1)}, f32[2,1024,64]{1,2,0:T(8,128)}, u32[]{:S(2)}) copy-start(f32[2,1024,64]{1,2,0:T(8,128)} %param.8) | copy-start | bytes 1572868
  17.4 1.0 %copy-start.2 = (bf16[2,1088,64]{1,2,0:T(8,128)(2,1)S(1)}, bf16[2,1088,64]{1,2,0:T(8,128)(2,1)}, u32[]{:S(2)}) copy-start(bf16[2,1088,64]{1,2,0:T(8,128)(2,1)} %param.9) | copy-start | bytes 835588
  18.3 25.2 %copy-start.1 = (bf16[512,512]{1,0:T(8,128)(2,1)S(1)}, bf16[512,512]{1,0:T(8,128)(2,1)}, u32[]{:S(2)}) copy-start(bf16[512,512]{1,0:T(8,128)(2,1)} %constant.26.clone.order) | copy-start | bytes 1572868
